TPU v7x, 128 devices: a whole 4x4x4 slice. The times are simulated.
128 devices in a mesh: row: 8 (over x, z_lo), col: 16 (over y, z_hi, core).
Axes of the slice: x: 4, y: 4, z: 4 (z_hi: 2, z_lo: 2; z = z_hi * 2 + z_lo), core: 2. Of those that a mesh axis runs over, the one named last changes fastest.
Arguments:
- front: float32 [16384, 16384], P('row', 'col'), may hold values from -6 to 6
- child_left: bfloat16 [14336, 256, 64], P(('row', 'col')), may hold values from -6 to 6
- child_right: bfloat16 [14336, 64, 256], P(('row', 'col')), may hold values from -0.75 to 0.75
- child_owner: int32 [14336, 1], P(('row', 'col')), may hold values from 0 to 127; in each aligned block of 112 rows (0 to 111, 112 to 223, ...) at most 2 rows name the same one
- child_slot: int32 [14336], P(('row', 'col')), may hold values from 0 to 31
- pivots: int32 [256], replicated, may hold values from 0 to 255, each once
- upper_inverse: float32 [256, 256], replicated, may hold values from -0.375 to 0.375
- lower_inverse: float32 [256, 256], replicated, may hold values from -0.375 to 0.375
- column_basis: float32 [256, 64], replicated, may hold values from -0.375 to 0.375
- row_basis: float32 [256, 64], replicated, may hold values from -0.375 to 0.375
- column_ranks: int32 [64], P('row'), may hold values from 32 to 64
- row_ranks: int32 [64], P('col'), may hold values from 32 to 64
Outputs:
- updated_front: float32 [16384, 16384], P('row', 'col')
Inputs may be any that keep to these rules, and one draw needn't show every extreme that they name: `child_owner`: owner device, numbered row index * 16 + col index; among the 112 child blocks of one device no owner is named more than 2 times, and exactly 2 times for some owner. `child_slot`: local block of the owner, numbered block row * 4 + block column. `pivots`: each of 0 to 255 once.
All inputs are finite; a program needn't handle non-finite values.
Results may differ from a plain program's by a relative error of at most 0.0003.
Values may be sent and summed in bfloat16 or wider, within the bound.
A program may use at most 192 MiB of HBM per device.

v0:
```python
import jax
import jax.numpy as jnp
from jax import lax
from jax.sharding import PartitionSpec as P

CAP = 2


def from_root(value, axis, source):
    kept = jnp.where(lax.axis_index(axis) == source, value, 0).astype(value.dtype)
    return lax.psum(kept, axis)


def shards(
    front,
    child_left,
    child_right,
    child_owner,
    child_slot,
    pivots,
    upper_inverse,
    lower_inverse,
    column_basis,
    row_basis,
    column_ranks,
    row_ranks,
):
    highest = lax.Precision.HIGHEST
    block_size = pivots.shape[0]
    rank_width = column_basis.shape[1]
    row_count = lax.axis_size("row")
    col_count = lax.axis_size("col")
    devices = row_count * col_count
    local_rows, local_cols = front.shape
    row_blocks = local_rows // block_size
    col_blocks = local_cols // block_size
    slot_total = devices * CAP
    owners = child_owner[:, 0]
    onehot = (owners[:, None] == jnp.arange(devices, dtype=jnp.int32)[None, :]).astype(jnp.int32)
    position = jnp.sum((jnp.cumsum(onehot, axis=0) - onehot) * onehot, axis=1)
    target = owners * CAP + position
    left_buffer = (
        jnp.zeros((slot_total, block_size, rank_width), jnp.bfloat16).at[target].set(child_left)
    )
    right_buffer = (
        jnp.zeros((slot_total, rank_width, block_size), jnp.bfloat16).at[target].set(child_right)
    )
    slot_buffer = jnp.full((slot_total,), -1, jnp.int32).at[target].set(child_slot)
    got_left, got_right, got_slots = (
        lax.all_to_all(
            left_buffer.reshape(devices, CAP, block_size, rank_width),
            ("row", "col"),
            split_axis=0,
            concat_axis=0,
            tiled=True,
        ),
        lax.all_to_all(
            right_buffer.reshape(devices, CAP, rank_width, block_size),
            ("row", "col"),
            split_axis=0,
            concat_axis=0,
            tiled=True,
        ),
        lax.all_to_all(
            slot_buffer.reshape(devices, CAP),
            ("row", "col"),
            split_axis=0,
            concat_axis=0,
            tiled=True,
        ),
    )
    groups = slot_total // 32
    got_left = got_left.reshape(groups, 32, block_size, rank_width)
    got_right = got_right.reshape(groups, 32, rank_width, block_size)
    got_slots = got_slots.reshape(groups, 32)

    def apply_group(front_grid, member):
        left_part, right_part, slot_ids = member
        product = jnp.einsum(
            "nbr,nrc->nbc", left_part, right_part, preferred_element_type=jnp.float32
        )
        safe_ids = jnp.maximum(slot_ids, 0)
        return (
            front_grid.at[safe_ids // col_blocks, :, safe_ids % col_blocks, :].add(product),
            None,
        )

    front_grid, unused = lax.scan(
        apply_group,
        front.reshape(row_blocks, block_size, col_blocks, block_size),
        (got_left, got_right, got_slots),
    )
    extended = front_grid.reshape(local_rows, local_cols)
    pivoted = jnp.take(extended[:block_size], pivots, axis=0)
    lower_panel = jnp.dot(extended[:, :block_size], upper_inverse, precision=highest)
    upper_panel = jnp.dot(lower_inverse, pivoted, precision=highest)
    col_mask = jnp.arange(rank_width)[None, :] < jnp.repeat(column_ranks, block_size)[:, None]
    row_mask = jnp.arange(rank_width)[:, None] < jnp.repeat(row_ranks, block_size)[None, :]
    column_local = jnp.where(col_mask, jnp.dot(lower_panel, column_basis, precision=highest), 0.0)
    row_local = jnp.where(row_mask, jnp.dot(row_basis.T, upper_panel, precision=highest), 0.0)
    column_factors = from_root(column_local, "col", 0)
    row_factors = from_root(row_local, "row", 0)
    coupling = jnp.dot(column_basis.T, row_basis, precision=highest)
    scaled = jnp.dot(column_factors, coupling, precision=highest)
    schur = extended - jnp.dot(scaled, row_factors, precision=highest)
    is_top = lax.axis_index("row") == 0
    is_left = lax.axis_index("col") == 0
    top_left = jnp.where(
        is_top,
        jnp.where(is_left, pivoted[:, :block_size], upper_panel[:, :block_size]),
        jnp.where(is_left, lower_panel[:block_size], schur[:block_size, :block_size]),
    )
    top_right = jnp.where(is_top, upper_panel[:, block_size:], schur[:block_size, block_size:])
    bottom_left = jnp.where(is_left, lower_panel[block_size:], schur[block_size:, :block_size])
    bottom_right = schur[block_size:, block_size:]
    upper_part = jnp.concatenate([top_left, top_right], axis=1)
    lower_part = jnp.concatenate([bottom_left, bottom_right], axis=1)
    return jnp.concatenate([upper_part, lower_part], axis=0)


def solution(mesh):
    in_specs = (
        P("row", "col"),
        P(("row", "col"), None, None),
        P(("row", "col"), None, None),
        P(("row", "col"), None),
        P(("row", "col")),
        P(),
        P(),
        P(),
        P(),
        P(),
        P("row"),
        P("col"),
    )
    out_specs = P("row", "col")
    return jax.shard_map(shards, mesh=mesh, in_specs=in_specs, out_specs=out_specs, check_vma=False)
```

profile of v0, /device:TPU:32, one launch (start us, length us, event | category | flops | bytes accessed | tf_op | source)
XLA Modules:
  0.0 753.2 jit_solution(17945025881526058434)
XLA Ops:
  7.5 0.8 select_reduce_fusion
  9.0 1.1 scatter_custom_fusion.1
  10.8 10.2 %all-to-all-start = ((s32[128,1,2]{2,1,0:T(1,128)}), s32[128,1,2]{2,1,0:T(1,128)S(1)}, u32[]{:S(2)}, u32[]{:S(2)}) async-start(s32[128,1,2]{2,1,0:T(1,128)} %bitcast.9), calls=%async_computation | async-start | bytes 131072 | tf_op jit(solution)/shard_map/all_to_all | solution.py:64
  21.0 4.5 broadcast_in_dim.49
  25.5 16.9 %scatter_fusion.1 = bf16[256,256,64]{1,2,0:T(8,128)(2,1)} fusion(bf16[256,256,64]{1,2,0:T(8,128)(2,1)} %broadcast_in_dim.49, s32[112]{0:T(128)S(1)} %fusion.17, bf16[112,256,64]{1,2,0:T(8,128)(2,1)} %param.15), kind=kCustom, calls=%fused_computation.3 | custom fusion | bytes 11010496 | tf_op jit(solution)/shard_map/scatter | solution.py:43
  42.4 10.2 %all-to-all-start.1 = ((bf16[128,2,256,64]{2,3,1,0:T(8,128)(2,1)}), bf16[128,2,256,64]{2,3,1,0:T(8,128)(2,1)}, u32[]{:S(2)}, u32[]{:S(2)}) async-start(bf16[128,2,256,64]{2,3,1,0:T(8,128)(2,1)} %bitcast.85), calls=%async_computation.1 | async-start | bytes 16777216 | tf_op jit(solution)/shard_map/all_to_all | solution.py:50
  52.7 4.3 broadcast_in_dim.50
  56.9 17.0 %scatter_fusion.2 = bf16[256,64,256]{2,1,0:T(8,128)(2,1)} fusion(bf16[256,64,256]{2,1,0:T(8,128)(2,1)} %broadcast_in_dim.50, s32[112]{0:T(128)S(1)} %fusion.17, bf16[112,64,256]{2,1,0:T(8,128)(2,1)} %param.16), kind=kCustom, calls=%fused_computation.4 | custom fusion | bytes 11010496 | tf_op jit(solution)/shard_map/scatter | solution.py:46
  74.0 84.6 %all-to-all-done.1 = bf16[128,2,256,64]{2,3,1,0:T(8,128)(2,1)} async-done(((bf16[128,2,256,64]{2,3,1,0:T(8,128)(2,1)}), bf16[128,2,256,64]{2,3,1,0:T(8,128)(2,1)}, u32[]{:S(2)}, u32[]{:S(2)}) %all-to-all-start.1) | async-done | bytes 8388640 | tf_op jit(solution)/shard_map/all_to_all | solution.py:50
  158.6 13.2 %all-to-all-start.2 = ((bf16[128,2,64,256]{3,2,1,0:T(8,128)(2,1)}), bf16[128,2,64,256]{3,2,1,0:T(8,128)(2,1)}, u32[]{:S(2)}, u32[]{:S(2)}) async-start(bf16[128,2,64,256]{3,2,1,0:T(8,128)(2,1)} %bitcast.86), calls=%async_computation.2 | async-start | bytes 16777216 | tf_op jit(solution)/shard_map/all_to_all | solution.py:57
  171.9 10.5 %reshape.168 = f32[8,256,4,256]{3,2,1,0:T(4,128)} reshape(f32[2048,1024]{1,0:T(8,128)} %param.14) | data formatting | bytes 16777216 | tf_op jit(solution)/shard_map/reshape | solution.py:90
  182.4 8.1 %copy.25 = f32[8,256,4,256]{3,1,2,0:T(8,128)} copy(f32[8,256,4,256]{3,2,1,0:T(4,128)} %reshape.168) | data formatting | bytes 16777216 | tf_op jit(solution)/shard_map/while | solution.py:88
  192.2 85.6 %all-to-all-done.2 = bf16[128,2,64,256]{3,2,1,0:T(8,128)(2,1)} async-done(((bf16[128,2,64,256]{3,2,1,0:T(8,128)(2,1)}), bf16[128,2,64,256]{3,2,1,0:T(8,128)(2,1)}, u32[]{:S(2)}, u32[]{:S(2)}) %all-to-all-start.2) | async-done | bytes 8388640 | tf_op jit(solution)/shard_map/all_to_all | solution.py:57
  277.7 192.8 %while.12 = (s32[]{:T(128)}, f32[8,256,4,256]{3,1,2,0:T(8,128)}, s32[8,32]{1,0:T(8,128)S(1)}, bf16[8,32,256,64]{2,3,1,0:T(8,128)(2,1)}, bf16[8,32,64,256]{3,2,1,0:T(8,128)(2,1)}, /*index=5*/s32[]{:T(128)}) while((s32[]{:T(128)}, f32[8,256,4,256]{3,1,2,0:T(8,128)}, s32[8,32]{1,0:T(8,128)S(1)}, bf16[8,32,256,64]{2,3,1,0:T(8,128)(2,1)}, ...), condition=%wide.region_7.8_spmd, body=%wide.region_5.7_spmd.sunk | while | flops 270533504 | bytes 35653192 | solution.py:88
  277.7 6.2 fusion.43
  284.0 17.7 %scatter_fusion = f32[8,256,4,256]{3,1,2,0:T(8,128)} fusion(f32[8,256,4,256]{3,1,2,0:T(8,128)} %get-tuple-element.132, s32[32]{0:T(128)S(1)} %fusion.42, f32[32,256,256]{2,1,0:T(8,128)} %fusion.43), kind=kCustom, calls=%fused_computation.1.clone.1 | custom fusion | flops 2097152 | bytes 25166080 | tf_op jit(solution)/shard_map/while/body/eval_jaxpr/scatter-add | solution.py:84
  301.7 6.2 fusion.43
  307.9 17.9 %scatter_fusion = f32[8,256,4,256]{3,1,2,0:T(8,128)} fusion(f32[8,256,4,256]{3,1,2,0:T(8,128)} %get-tuple-element.132, s32[32]{0:T(128)S(1)} %fusion.42, f32[32,256,256]{2,1,0:T(8,128)} %fusion.43), kind=kCustom, calls=%fused_computation.1.clone.1 | custom fusion | flops 2097152 | bytes 25166080 | tf_op jit(solution)/shard_map/while/body/eval_jaxpr/scatter-add | solution.py:84
  325.8 6.2 fusion.43
  332.0 17.7 %scatter_fusion = f32[8,256,4,256]{3,1,2,0:T(8,128)} fusion(f32[8,256,4,256]{3,1,2,0:T(8,128)} %get-tuple-element.132, s32[32]{0:T(128)S(1)} %fusion.42, f32[32,256,256]{2,1,0:T(8,128)} %fusion.43), kind=kCustom, calls=%fused_computation.1.clone.1 | custom fusion | flops 2097152 | bytes 25166080 | tf_op jit(solution)/shard_map/while/body/eval_jaxpr/scatter-add | solution.py:84
  349.8 6.2 fusion.43
  356.0 17.9 %scatter_fusion = f32[8,256,4,256]{3,1,2,0:T(8,128)} fusion(f32[8,256,4,256]{3,1,2,0:T(8,128)} %get-tuple-element.132, s32[32]{0:T(128)S(1)} %fusion.42, f32[32,256,256]{2,1,0:T(8,128)} %fusion.43), kind=kCustom, calls=%fused_computation.1.clone.1 | custom fusion | flops 2097152 | bytes 25166080 | tf_op jit(solution)/shard_map/while/body/eval_jaxpr/scatter-add | solution.py:84
  373.9 6.2 fusion.43
  380.1 17.9 %scatter_fusion = f32[8,256,4,256]{3,1,2,0:T(8,128)} fusion(f32[8,256,4,256]{3,1,2,0:T(8,128)} %get-tuple-element.132, s32[32]{0:T(128)S(1)} %fusion.42, f32[32,256,256]{2,1,0:T(8,128)} %fusion.43), kind=kCustom, calls=%fused_computation.1.clone.1 | custom fusion | flops 2097152 | bytes 25166080 | tf_op jit(solution)/shard_map/while/body/eval_jaxpr/scatter-add | solution.py:84
  398.0 6.2 fusion.43
  404.3 17.9 %scatter_fusion = f32[8,256,4,256]{3,1,2,0:T(8,128)} fusion(f32[8,256,4,256]{3,1,2,0:T(8,128)} %get-tuple-element.132, s32[32]{0:T(128)S(1)} %fusion.42, f32[32,256,256]{2,1,0:T(8,128)} %fusion.43), kind=kCustom, calls=%fused_computation.1.clone.1 | custom fusion | flops 2097152 | bytes 25166080 | tf_op jit(solution)/shard_map/while/body/eval_jaxpr/scatter-add | solution.py:84
  422.2 6.2 fusion.43
  428.4 18.1 %scatter_fusion = f32[8,256,4,256]{3,1,2,0:T(8,128)} fusion(f32[8,256,4,256]{3,1,2,0:T(8,128)} %get-tuple-element.132, s32[32]{0:T(128)S(1)} %fusion.42, f32[32,256,256]{2,1,0:T(8,128)} %fusion.43), kind=kCustom, calls=%fused_computation.1.clone.1 | custom fusion | flops 2097152 | bytes 25166080 | tf_op jit(solution)/shard_map/while/body/eval_jaxpr/scatter-add | solution.py:84
  446.5 6.2 fusion.43
  452.8 17.8 %scatter_fusion = f32[8,256,4,256]{3,1,2,0:T(8,128)} fusion(f32[8,256,4,256]{3,1,2,0:T(8,128)} %get-tuple-element.132, s32[32]{0:T(128)S(1)} %fusion.42, f32[32,256,256]{2,1,0:T(8,128)} %fusion.43), kind=kCustom, calls=%fused_computation.1.clone.1 | custom fusion | flops 2097152 | bytes 25166080 | tf_op jit(solution)/shard_map/while/body/eval_jaxpr/scatter-add | solution.py:84
  470.5 10.4 %copy.28 = f32[8,256,4,256]{1,0,3,2:T(8,128)} copy(f32[8,256,4,256]{3,1,2,0:T(8,128)} %get-tuple-element.73) | data formatting | bytes 16777216 | tf_op jit(solution)/shard_map/while | solution.py:88
  480.9 1.3 slice.36
  482.2 7.5 copy.33
  489.8 3.4 copy-done.1
  493.1 2.0 fusion.11
  495.2 2.3 fusion.10
  498.7 2.0 gather_fusion
  500.8 1.6 copy.27
  502.4 1.0 copy-done.2
  503.4 2.0 fusion.20
  505.4 1.8 fusion.14
  508.0 138.0 %all-reduce.3.cloned.1.call-done = f32[2048,64]{0,1:T(8,128)} async-done(((f32[2048,64]{0,1:T(8,128)}), f32[2048,64]{0,1:T(8,128)}) %all-reduce.3.cloned.1.call-update) | async-done | bytes 524304 | tf_op jit(solution)/shard_map/psum | solution.py:11
  646.0 2.5 fusion.22
  648.5 73.1 %all-reduce.5.cloned.1.call-done = f32[64,1024]{1,0:T(8,128)} async-done(((f32[64,1024]{1,0:T(8,128)}), f32[64,1024]{1,0:T(8,128)}) %all-reduce.5.cloned.1.call-update) | async-done | bytes 262160 | tf_op jit(solution)/shard_map/psum | solution.py:11
  721.6 9.5 %convolution_subtract_fusion = f32[2048,1024]{0,1:T(8,128)S(1)} fusion(f32[2048,1024]{0,1:T(8,128)} %bitcast.88, f32[2048,64]{0,1:T(8,128)} %fusion.22, f32[64,1024]{1,0:T(8,128)} %all-reduce.5.cloned.1.call-done), kind=kOutput, calls=%fused_computation.24 | convolution fusion | flops 1612709888 | bytes 17563648 | tf_op jit(solution)/shard_map/dot_general | solution.py:105
  731.1 1.0 fusion.15
  733.1 4.0 maximum_maximum_fusion
  737.1 9.2 %copy.29 = f32[2048,1024]{1,0:T(8,128)} copy(f32[2048,1024]{0,1:T(8,128)} %maximum_maximum_fusion) | data formatting | bytes 16777216 | tf_op jit(solution)/shard_map/concatenate | solution.py:118
  (48 shorter events, 7.1 us)
Async XLA Ops:
  6.5 486.6 %copy-start = (f32[256,256]{1,0:T(8,128)S(1)}, f32[256,256]{1,0:T(8,128)}, u32[]{:S(2)}) copy-start(f32[256,256]{1,0:T(8,128)} %param.20) | copy-start | bytes 786436
  10.8 31.6 %all-to-all-start = ((s32[128,1,2]{2,1,0:T(1,128)}), s32[128,1,2]{2,1,0:T(1,128)S(1)}, u32[]{:S(2)}, u32[]{:S(2)}) async-start(s32[128,1,2]{2,1,0:T(1,128)} %bitcast.9), calls=%async_computation | async-start | bytes 131072 | tf_op jit(solution)/shard_map/all_to_all | solution.py:64
  42.4 116.2 %all-to-all-start.1 = ((bf16[128,2,256,64]{2,3,1,0:T(8,128)(2,1)}), bf16[128,2,256,64]{2,3,1,0:T(8,128)(2,1)}, u32[]{:S(2)}, u32[]{:S(2)}) async-start(bf16[128,2,256,64]{2,3,1,0:T(8,128)(2,1)} %bitcast.85), calls=%async_computation.1 | async-start | bytes 16777216 | tf_op jit(solution)/shard_map/all_to_all | solution.py:50
  158.6 119.1 %all-to-all-start.2 = ((bf16[128,2,64,256]{3,2,1,0:T(8,128)(2,1)}), bf16[128,2,64,256]{3,2,1,0:T(8,128)(2,1)}, u32[]{:S(2)}, u32[]{:S(2)}) async-start(bf16[128,2,64,256]{3,2,1,0:T(8,128)(2,1)} %bitcast.86), calls=%async_computation.2 | async-start | bytes 16777216 | tf_op jit(solution)/shard_map/all_to_all | solution.py:57
  171.8 474.2 %all-reduce.3.cloned.1.call-start = ((), (), s32[]{:S(2)}) async-start(), calls=%async_computation.3 | async-start | bytes 1048576 | tf_op jit(solution)/shard_map/psum | solution.py:11
  182.4 8.1 %copy-start.6 = (s32[8]{0:T(128)S(1)}, s32[8]{0:T(128)}, u32[]{:S(2)}) copy-start(s32[8]{0:T(128)} %param.24) | copy-start | bytes 100
  182.4 8.2 %copy-start.7 = (s32[4]{0:T(128)S(1)}, s32[4]{0:T(128)}, u32[]{:S(2)}) copy-start(s32[4]{0:T(128)} %param.25) | copy-start | bytes 52
  182.4 8.3 %copy-start.5 = (s32[256]{0:T(256)S(1)}, s32[256]{0:T(256)}, u32[]{:S(2)}) copy-start(s32[256]{0:T(256)} %param.19) | copy-start | bytes 3076
  482.2 13.0 %copy-start.3 = (f32[256,64]{0,1:T(8,128)S(1)}, f32[256,64]{0,1:T(8,128)}, u32[]{:S(2)}) copy-start(f32[256,64]{0,1:T(8,128)} %param.22) | copy-start | bytes 196612
  489.7 3.4 copy-start.1
  497.5 224.1 %all-reduce.5.cloned.1.call-start = ((), (), s32[]{:S(2)}) async-start(), calls=%async_computation.4 | async-start | bytes 524288 | tf_op jit(solution)/shard_map/psum | solution.py:11
  498.7 6.7 copy-start.4
  502.4 1.0 copy-start.2
Sparse Core Ops, SparseCore 0:
  497.7 148.3 all-reduce.2
  648.6 72.9 all-reduce.4
where the time goes:
time: 758 us; the launch traced here: 753 us
  waiting for transfers between devices  381 us (50%)
  other arithmetic  152 us (20%)
  local copies, waits for them, and re-layouts  102 us (13%)
  matrix products  70.8 us (9%)
  starting transfers between devices  33.9 us (4%)
  between operations  13.6 us (2%)
    psum x2, waiting for transfers between devices, from_root(): return lax.psum(kept, axis)  211 us
    scatter-add x8, other arithmetic, apply_group(): front_grid.at[safe_ids // col_blocks, :, safe_ids % col_blocks, :]  143 us
    all_to_all x1, waiting for transfers between devices, shards(): lax.all_to_all(right_buffer.reshape(devices, CAP, rank_width, block_size)...  85.6 us
    all_to_all x1, waiting for transfers between devices, shards(): lax.all_to_all(left_buffer.reshape(devices, CAP, block_size, rank_width),...  84.6 us
    dot_general x8, matrix products, apply_group(): jnp.einsum('nbr,nrc->nbc', left_part, right_part, preferred_element_type=...  49.8 us
    while x2, local copies, waits for them, and re-layouts, shards(): lax.scan(apply_group, front.reshape(row_blocks, block_size, col_blocks, b...  18.5 us
    scatter x1, local copies, waits for them, and re-layouts, shards(): jnp.zeros((slot_total, rank_width, block_size), jnp.bfloat16).at[target]  17 us
    scatter x1, local copies, waits for them, and re-layouts, shards(): jnp.zeros((slot_total, block_size, rank_width), jnp.bfloat16).at[target]  16.9 us
  transfers between devices with their start and end apart: 5, of which 4 were waited for; matrix products, arithmetic and copies ran while one was open for 10% of the time, Pallas kernels for 0%

commit v1 on v0

v1 whole, which is shorter than its diff:
```python
import functools

import jax
import jax.numpy as jnp
from jax import lax
from jax.experimental import pallas as pl
from jax.experimental.pallas import tpu as pltpu
from jax.sharding import PartitionSpec as P

MESH = pl.DeviceIdType.MESH
HBM = pl.BlockSpec(memory_space=pl.ANY)
SMEM = pl.BlockSpec(memory_space=pltpu.SMEM)
VMEM = pl.BlockSpec(memory_space=pltpu.VMEM)
DMA = pltpu.SemaphoreType.DMA
CAP = 2
STACK = 4
STRIDE = 37
RING = 4
CHIPS = RING**3
LEAD = 16
LIMIT = 56 * 1024 * 1024
HIGHEST = lax.Precision.HIGHEST


def dot(a, b, dims=((1,), (0,)), precision=None):
    return lax.dot_general(
        a, b, (dims, ((), ())), precision=precision, preferred_element_type=jnp.float32
    )


def pack_kernel(
    devices, owner, owner_row, slot_row, left, right, packed, table, staged, named, placed, in_sem,
    out_sem,
):
    count, rank = left.shape[0], left.shape[1]
    chips = devices // 2
    chunks = in_sem.shape[0]
    each = count // chunks

    def load(k):
        part = pl.ds(k * each, each)
        return (
            pltpu.make_async_copy(left.at[part], staged.at[part, pl.ds(0, rank)], in_sem.at[k, 0]),
            pltpu.make_async_copy(right.at[part], staged.at[part, pl.ds(rank, rank)], in_sem.at[k, 1]),
        )

    for k in range(chunks):
        for copy in load(k):
            copy.start()

    def clear(o, c):
        named[o] = 0
        placed[o] = 0
        return c

    lax.fori_loop(0, devices, clear, 0, unroll=8)

    def tally(i, c):
        named[owner[i]] += 1
        return c

    lax.fori_loop(0, count, tally, 0, unroll=4)

    shape = (devices, 1, count)
    place = lax.broadcasted_iota(jnp.int32, shape, 2)
    device = lax.broadcasted_iota(jnp.int32, shape, 0)
    owners = owner_row[...][None]
    code = (place * 64 + slot_row[...][None]).astype(jnp.float32)

    def ends(which):
        least = jnp.min(jnp.where(which, code, 65536.0), axis=2, keepdims=True)
        most = jnp.max(jnp.where(which, code, -1.0), axis=2, keepdims=True)
        return least, most

    least, most = ends(owners == device)
    low_least, low_most = ends(owners == device - (device & 1))
    core = device[:, :, 0:1] & 1
    first = jnp.where(most >= 0.0, least.astype(jnp.int32) & 63, -1)
    second = jnp.where(most > least, most.astype(jnp.int32) & 63, -1)
    late = jnp.logical_and(core == 1, low_most > low_least)
    last = jnp.where(late, second, -1)
    flag = jnp.max(last.astype(jnp.float32), axis=0, keepdims=True).astype(jnp.int32)
    lane = lax.broadcasted_iota(jnp.int32, table.shape, 2)
    line = jnp.where(lane == 0, first, jnp.where(lane == 1, jnp.where(late, -1, second), -1))
    table[...] = jnp.where(lane == 2, last, jnp.where(lane == 3, flag, line))

    for k in range(chunks):
        for copy in load(k):
            copy.wait()

        def send(i, c):
            o = owner[i]
            p = placed[o]
            placed[o] = 1
            chip = o // 2
            late = jnp.logical_and(o % 2 == 1, named[o - o % 2] == 2)
            extra = jnp.where(late, devices + chips + chip, devices + chip)
            at = jnp.where(p == 0, o, extra)
            pltpu.make_async_copy(staged.at[i], packed.at[at], out_sem).start()
            return c

        lax.fori_loop(k * each, (k + 1) * each, send, 0)
    pltpu.make_async_copy(staged, packed.at[pl.ds(0, count)], out_sem).wait()


def pack(owner, slots, left, right, devices):
    count, rank, size = left.shape
    return pl.pallas_call(
        functools.partial(pack_kernel, devices),
        out_shape=(
            jax.ShapeDtypeStruct((2 * devices, 2 * rank, size), left.dtype),
            jax.ShapeDtypeStruct((devices, 1, 128), jnp.int32),
        ),
        in_specs=[SMEM, VMEM, VMEM, HBM, HBM],
        out_specs=(HBM, VMEM),
        scratch_shapes=[
            pltpu.VMEM((count, 2 * rank, size), left.dtype),
            pltpu.SMEM((devices,), jnp.int32),
            pltpu.SMEM((devices,), jnp.int32),
            DMA((4, 2)),
            DMA,
        ],
        compiler_params=pltpu.CompilerParams(vmem_limit_bytes=LIMIT),
        name="pack",
    )(owner, owner[None, :], slots[None, :], left, right)


def position():
    r, q = lax.axis_index("row"), lax.axis_index("col")
    return r // 2, q // 4, lax.rem(q // 2, 2) * 2 + lax.rem(r, 2), lax.rem(q, 2)


def place_of(x, y, z, core):
    x, y, z = lax.rem(x, RING), lax.rem(y, RING), lax.rem(z, RING)
    return x * 2 + lax.rem(z, 2), y * 4 + (z // 2) * 2 + core


def step_of(k):
    d = lax.rem(k * STRIDE, CHIPS)
    steps = (d // (RING * RING), lax.rem(d // RING, RING), lax.rem(d, RING))
    far = [s // 2 - s // 3 for s in steps]
    both = far[0] + far[1] + far[2] > 0
    up = 1 - lax.rem(steps[0] + steps[1] + steps[2], 2)
    return d, steps, far, both, up


def legs(steps, far, up):
    ahead = [f * (3 - 2 * up) for f in far]
    return ahead, [s + 4 - a for s, a in zip(steps, ahead)]


def far_count():
    return sum(2 in (d // 16, d // 4 % 4, d % 4) for d in range(1, CHIPS))


def remote(src, dst, send, recv, device):
    return pltpu.make_async_remote_copy(
        src_ref=src, dst_ref=dst, send_sem=send, recv_sem=recv, device_id=device,
        device_id_type=MESH,
    )


def exchange_kernel(
    n_row, n_col, packed, table, got, got_table, relay, table_sems, block_sems, relay_sem,
    shared_sem, own_sem,
):
    devices = n_row * n_col
    x, y, z, core = position()
    mine = place_of(x, y, z, core)
    me = mine[0] * n_col + mine[1]
    sibling = place_of(x, y, z, 1 - core)
    sibling_id = sibling[0] * n_col + sibling[1]
    chip = me // 2
    barrier = pltpu.get_barrier_semaphore()
    a_send, a_recv, t_send, r_send, f_send, f_recv = [block_sems.at[i] for i in range(6)]

    own = (
        pltpu.make_async_copy(packed.at[me], got.at[0, me], own_sem.at[0]),
        pltpu.make_async_copy(packed.at[devices + chip], got.at[1, me], own_sem.at[1]),
        pltpu.make_async_copy(table.at[me], got_table.at[me], own_sem.at[2]),
    )
    for copy in own:
        copy.start()

    def others(body):
        def one(k, carry):
            o = lax.rem(me + k, devices)
            body(o, (o // n_col, lax.rem(o, n_col)))
            return carry

        lax.fori_loop(1, devices, one, 0)

    others(lambda o, at: pl.semaphore_signal(barrier, 1, device_id=at, device_id_type=MESH))
    pl.semaphore_wait(barrier, devices - 1)

    def at_step(steps, core):
        return place_of(x + steps[0], y + steps[1], z + steps[2], core)

    def number(device):
        return device[0] * n_col + device[1]

    def kinds(up):
        return (
            (0, 0, 1, a_send, lambda d: a_recv),
            (0, 1, 0, a_send, lambda d: a_recv),
            (1, core, up, t_send, lambda d: shared_sem.at[d]),
        )

    def source_block(layer, target):
        return packed.at[devices + number(target) // 2 if layer else number(target)]

    def first_leg(k):
        d, steps, far, both, up = step_of(k)
        for i, (layer, side, way, send, recv) in enumerate(kinds(up)):
            first, second = legs(steps, far, way)
            remote(
                source_block(layer, at_step(steps, side)), relay.at[i * CHIPS + d], send,
                relay_sem.at[i * CHIPS + d], at_step(first, core),
            ).start()

    def direct(k):
        d, steps, far, both, up = step_of(k)
        for layer, side, way, send, recv in kinds(up):
            target = at_step(steps, side)
            remote(source_block(layer, target), got.at[layer, me], send, recv(d), target).start()

    def second_leg(k):
        d, steps, far, both, up = step_of(k)

        @pl.when(both)
        def _():
            for i, (layer, side, way, send, recv) in enumerate(kinds(up)):
                first, second = legs(steps, far, way)
                source = number(at_step([4 - f for f in first], core))
                target = at_step(second, side)
                held = relay.at[i * CHIPS + d]
                remote(held, held, r_send, relay_sem.at[i * CHIPS + d], target).wait_recv()
                remote(held, got.at[layer, source], r_send, recv(d), target).start()

    def hand_over(k):
        d, steps, far, both, up = step_of(k)
        source = number(place_of(x + RING - steps[0], y + RING - steps[1], z + RING - steps[2], core))
        remote(got.at[1, source], got.at[1, source], f_send, shared_sem.at[d], sibling).wait_recv()
        remote(got.at[1, source], got.at[1, source], f_send, f_recv, sibling).start()

    others(
        lambda o, at: remote(
            table.at[o], got_table.at[me], table_sems.at[0], table_sems.at[1], at
        ).start()
    )
    remote(packed.at[sibling_id], got.at[0, me], a_send, a_recv, sibling).start()
    remote(packed.at[devices + chip], got.at[1, me], f_send, f_recv, sibling).start()
    def far_step(k, carry):
        both = step_of(k)[3]

        @pl.when(both)
        def _():
            first_leg(k)

        return carry

    def far_relay(k, carry):
        far_step(k, carry)
        second_leg(k - LEAD)
        return carry

    def relay_only(k, carry):
        second_leg(k)
        return carry

    def near_step(k, carry):
        both = step_of(k)[3]
        pl.when(jnp.logical_not(both))(lambda: direct(k))
        return carry

    def end(k, carry):
        hand_over(k)
        return carry

    lax.fori_loop(1, LEAD + 1, far_step, 0)
    lax.fori_loop(LEAD + 1, CHIPS, far_relay, 0)
    lax.fori_loop(1, CHIPS // 2, near_step, 0)
    lax.fori_loop(CHIPS - LEAD, CHIPS, relay_only, 0)
    lax.fori_loop(CHIPS // 2, CHIPS, near_step, 0)
    lax.fori_loop(1, CHIPS, end, 0)
    for copy in own:
        copy.wait()

    def settle(ref, count, sem):
        part = ref.at[pl.ds(0, count)]
        pltpu.make_async_copy(part, part, sem).wait()

    settle(got_table, devices - 1, table_sems.at[1])
    settle(table, devices - 1, table_sems.at[0])
    settle(got.at[0], devices - 1, a_recv)
    settle(got.at[1], CHIPS, f_recv)
    settle(packed, devices - 1, a_send)
    settle(packed, CHIPS - 1, t_send)
    settle(relay, 3 * far_count(), r_send)
    settle(got.at[1], CHIPS, f_send)


def exchange(packed, table, n_row, n_col):
    devices = n_row * n_col
    block = packed.shape[1:]
    return pl.pallas_call(
        functools.partial(exchange_kernel, n_row, n_col),
        out_shape=(
            jax.ShapeDtypeStruct((3, devices) + block, packed.dtype),
            jax.ShapeDtypeStruct(table.shape, table.dtype),
            jax.ShapeDtypeStruct((3 * CHIPS,) + block, packed.dtype),
        ),
        in_specs=[HBM, HBM],
        out_specs=(HBM, HBM, HBM),
        scratch_shapes=[DMA((2,)), DMA((6,)), DMA((3 * CHIPS,)), DMA((CHIPS,)), DMA((3,))],
        compiler_params=pltpu.CompilerParams(collective_id=2, has_side_effects=True),
        name="exchange",
    )(packed, table)


def last_kernel(n_row, n_col, packed, got_in, got, relay, sems, relay_sem, own_sem):
    devices = n_row * n_col
    x, y, z, core = position()
    mine = place_of(x, y, z, core)
    me = mine[0] * n_col + mine[1]
    first_block = devices + CHIPS
    barrier = pltpu.get_barrier_semaphore()

    def at_step(steps, core):
        return place_of(x + steps[0], y + steps[1], z + steps[2], core)

    def number(device):
        return device[0] * n_col + device[1]

    def greet(at):
        pl.semaphore_signal(barrier, 1, device_id=at, device_id_type=MESH)

    def near(k, carry):
        d, steps, far, both, up = step_of(k)

        @pl.when(jnp.logical_and(core == 1, jnp.logical_not(both)))
        def _():
            greet(at_step(steps, 0))
            greet(at_step(steps, 1))

        return carry

    def relayed(k, carry):
        bits = (k // 8, lax.rem(k // 4, 2), lax.rem(k // 2, 2))
        way = lax.rem(k, 2)

        @pl.when(jnp.logical_and(core == 0, k != 15))
        def _():
            greet(at_step([b * (3 - 2 * way) for b in bits], 0))

        return carry

    lax.fori_loop(1, CHIPS, near, 0)
    lax.fori_loop(2, 16, relayed, 0)

    @pl.when(core == 1)
    def _():
        greet(place_of(x, y, z, 0))
        pl.semaphore_wait(barrier, 26)

    @pl.when(core == 0)
    def _():
        pl.semaphore_wait(barrier, 26 + 13 + 1)

    def block_for(target):
        return packed.at[first_block + number(target) // 2]

    def first_leg(k, carry):
        d, steps, far, both, up = step_of(k)

        @pl.when(both)
        def _():
            first, second = legs(steps, far, up)
            remote(
                block_for(at_step(steps, 1)), relay.at[d], sems.at[0], relay_sem.at[d],
                at_step(first, core),
            ).start()

        return carry

    def direct(k, carry):
        d, steps, far, both, up = step_of(k)

        @pl.when(jnp.logical_not(both))
        def _():
            target = at_step(steps, 1)
            remote(block_for(target), got.at[2, me], sems.at[0], sems.at[1], target).start()

        return carry

    def second_leg(k, carry):
        d, steps, far, both, up = step_of(k)

        @pl.when(both)
        def _():
            first, second = legs(steps, far, up)
            source = number(at_step([4 - f for f in first], core))
            target = at_step(second, 1)
            held = relay.at[d]
            remote(held, held, sems.at[2], relay_sem.at[d], target).wait_recv()
            remote(held, got.at[2, source], sems.at[2], sems.at[1], target).start()

        return carry

    lax.fori_loop(1, CHIPS, first_leg, 0)
    lax.fori_loop(1, CHIPS, direct, 0)
    lax.fori_loop(1, CHIPS, second_leg, 0)

    def settle(ref, count, sem):
        part = ref.at[pl.ds(0, count)]
        pltpu.make_async_copy(part, part, sem).wait()

    settle(relay, far_count(), sems.at[2])

    @pl.when(core == 0)
    def _():
        to = place_of(x, y, z, 1)
        remote(packed.at[first_block + me // 2], got.at[2, me], sems.at[0], sems.at[1], to).start()
        settle(packed, CHIPS, sems.at[0])

    @pl.when(core == 1)
    def _():
        own = pltpu.make_async_copy(packed.at[first_block + me // 2], got.at[2, me], own_sem)
        own.start()
        own.wait()
        settle(packed, CHIPS - 1, sems.at[0])
        settle(got.at[2], devices - 1, sems.at[1])


def exchange_last(packed, got, n_row, n_col):
    return pl.pallas_call(
        functools.partial(last_kernel, n_row, n_col),
        out_shape=(
            jax.ShapeDtypeStruct(got.shape, got.dtype),
            jax.ShapeDtypeStruct((CHIPS,) + packed.shape[1:], packed.dtype),
        ),
        in_specs=[HBM, HBM],
        out_specs=(HBM, HBM),
        input_output_aliases={1: 0},
        scratch_shapes=[DMA((3,)), DMA((CHIPS,)), DMA],
        compiler_params=pltpu.CompilerParams(collective_id=3, has_side_effects=True),
        name="exchange_last",
    )(packed, got)[0]


def fetch_target(t, at, total, counts, order, base, got, buffer, sem):
    base[t] = at

    def one(e, c):
        pltpu.make_async_copy(got.at[order[t * total + e]], buffer.at[at + e], sem).start()
        return c

    lax.fori_loop(0, counts[t], one, 0)
    return at + counts[t]


def await_target(t, counts, got, buffer, sem):
    def one(e, c):
        pltpu.make_async_copy(got.at[0], buffer.at[0], sem).wait()
        return c

    lax.fori_loop(0, counts[t], one, 0)


def product(t, e, counts, base, buffer):
    rank = buffer.shape[1] // 2
    n, begin = counts[t], base[t]
    picked = [
        jnp.where(e * STACK + k < n, begin + e * STACK + k, buffer.shape[0] - 1) for k in range(STACK)
    ]
    lefts = jnp.concatenate([buffer[s, 0:rank, :] for s in picked], axis=0)
    rights = jnp.concatenate([buffer[s, rank:, :] for s in picked], axis=0)
    return dot(lefts, rights, ((0,), (0,)))


def add_rest(t, counts, base, buffer, sum_ref, rows, cols):
    def chunk(e, c):
        sum_ref[rows, cols] += product(t, e, counts, base, buffer)
        return c

    lax.fori_loop(1, (counts[t] + STACK - 1) // STACK, chunk, 0)


def split(x):
    high = x.astype(jnp.bfloat16)
    return high, (x - high.astype(jnp.float32)).astype(jnp.bfloat16)


def permutation(pivots):
    size = pivots.shape[1]
    places = lax.broadcasted_iota(jnp.int32, (size, size), 0)
    return (places == pivots).astype(jnp.float32)


def panel_kernel(
    total, table, got, front, pivots, upper_inverse, lower_inverse, column_basis, row_basis,
    column_ranks, row_ranks, a_out, b_out, counts, order, left_sum, top_sum, buffer, top_weights,
    left_weights, coupling, base, sem, front_sem,
):
    size, rank = upper_inverse.shape[0], column_basis.shape[0]
    row_blocks, col_blocks = front.shape[0] // size, front.shape[1] // size
    targets = row_blocks * col_blocks
    devices = table.shape[0]
    is_top, is_left = lax.axis_index("row") == 0, lax.axis_index("col") == 0
    load_left = pltpu.make_async_copy(front.at[:, pl.ds(0, size)], left_sum, front_sem.at[0])
    load_top = pltpu.make_async_copy(front.at[pl.ds(0, size)], top_sum, front_sem.at[1])
    pl.when(is_left)(load_left.start)
    pl.when(is_top)(load_top.start)

    for t in range(targets + 1):
        counts[t] = 0

    def note(s, p):
        t = table[s, 0, p]
        t = jnp.where(t < 0, targets, t)
        n = counts[t]
        order[t * total + n] = p * devices + s
        counts[t] = n + 1

    def tally(s, flags):
        note(s, 0)
        note(s, 1)
        return jnp.maximum(flags, table[s, 0, 3])

    def tally_last(s, c):
        note(s, 2)
        return c

    flags = lax.fori_loop(0, devices, tally, -1, unroll=4)
    lax.fori_loop(0, jnp.where(flags >= 0, devices, 0), tally_last, 0)

    @pl.when(jnp.logical_or(is_top, is_left))
    def _():
        buffer[buffer.shape[0] - 1] = jnp.zeros(buffer.shape[1:], buffer.dtype)

        def fetch(t, at):
            return fetch_target(t, at, total, counts, order, base, got, buffer, sem)

        def fetch_left(i, at):
            return fetch(i * col_blocks, at)

        at = lax.fori_loop(0, jnp.where(is_left, row_blocks, 0), fetch_left, 0)
        lax.fori_loop(jnp.where(is_left, 1, 0), jnp.where(is_top, col_blocks, 0), fetch, at)

    @pl.when(is_top)
    def _():
        weights = dot(row_basis[...], lower_inverse[...], precision=HIGHEST)
        weights = dot(weights, permutation(pivots[...]), ((1,), (1,)), precision=HIGHEST)
        top_weights[0:rank] = weights
        top_weights[rank:] = weights

    @pl.when(is_left)
    def _():
        left_weights[...] = dot(
            upper_inverse[...], column_basis[...], ((1,), (1,)), precision=HIGHEST
        )
        coupled = dot(column_basis[...], row_basis[...], ((1,), (1,)), precision=HIGHEST)
        coupling[...] = jnp.concatenate([coupled, coupled], axis=1)

    @pl.when(jnp.logical_or(is_top, is_left))
    def _():
        def ready(t):
            await_target(t, counts, got, buffer, sem)

        def ready_left(i, c):
            ready(i * col_blocks)
            return c

        def ready_top(t, c):
            ready(t)
            return c

        lax.fori_loop(0, jnp.where(is_left, row_blocks, 0), ready_left, 0)
        lax.fori_loop(jnp.where(is_left, 1, 0), jnp.where(is_top, col_blocks, 0), ready_top, 0)

    @pl.when(is_top)
    def _():
        row = lax.broadcasted_iota(jnp.int32, (2 * rank, size), 0)
        load_top.wait()
        for j in range(col_blocks):
            cols = slice(j * size, (j + 1) * size)
            top_sum[:, cols] += product(j, 0, counts, base, buffer)
        for j in range(col_blocks):
            add_rest(j, counts, base, buffer, top_sum, slice(0, size), slice(j * size, (j + 1) * size))
        for j in range(col_blocks):
            cols = slice(j * size, (j + 1) * size)
            factor = dot(top_weights[...], top_sum[:, cols], precision=HIGHEST)
            factor = jnp.where(lax.rem(row, rank) < row_ranks[j], factor, 0.0)
            high, low = split(factor)
            value = jnp.where(row < rank, high.astype(jnp.float32), low.astype(jnp.float32))
            for h in range(size // 128):
                b_out[j * (size // 128) + h] = value[:, h * 128 : (h + 1) * 128].astype(jnp.bfloat16)

    @pl.when(is_left)
    def _():
        lane = lax.broadcasted_iota(jnp.int32, (size, 2 * rank), 1)
        load_left.wait()

        def add(i, c):
            rows = pl.ds(pl.multiple_of(i * size, size), size)
            left_sum[rows, :] += product(i * col_blocks, 0, counts, base, buffer)
            return c

        lax.fori_loop(0, row_blocks, add, 0, unroll=4)

        def add_more(i, c):
            rows = pl.ds(pl.multiple_of(i * size, size), size)
            add_rest(i * col_blocks, counts, base, buffer, left_sum, rows, slice(0, size))
            return c

        lax.fori_loop(0, row_blocks, add_more, 0)

        def block(i, c):
            rows = pl.ds(pl.multiple_of(i * size, size), size)
            factor = dot(left_sum[rows, :], left_weights[...], precision=HIGHEST)
            factor = jnp.where(lane[:, 0:rank] < column_ranks[i], factor, 0.0)
            high, low = split(dot(factor, coupling[...], precision=HIGHEST))
            value = jnp.where(lane < rank, high.astype(jnp.float32), low.astype(jnp.float32))
            for h in range(size // 128):
                a_out[i * (size // 128) + h] = value[h * 128 : (h + 1) * 128].astype(jnp.bfloat16)
            return c

        lax.fori_loop(0, row_blocks, block, 0, unroll=4)


def panel(
    table, got, front, pivots, upper_inverse, lower_inverse, column_basis, row_basis, column_ranks,
    row_ranks,
):
    depth, size = got.shape[1:]
    total = table.shape[0] * CAP
    rows, cols = front.shape
    targets = (rows // size) * (cols // size)
    return pl.pallas_call(
        functools.partial(panel_kernel, total),
        out_shape=(
            jax.ShapeDtypeStruct((rows // 128, 128, 128), jnp.bfloat16),
            jax.ShapeDtypeStruct((cols // 128, 128, 128), jnp.bfloat16),
            jax.ShapeDtypeStruct((targets + 1,), jnp.int32),
            jax.ShapeDtypeStruct(((targets + 2) * total,), jnp.int32),
        ),
        in_specs=[SMEM, HBM, HBM, VMEM, VMEM, VMEM, VMEM, VMEM, SMEM, SMEM],
        out_specs=(VMEM, VMEM, SMEM, SMEM),
        scratch_shapes=[
            pltpu.VMEM((rows, size), jnp.float32),
            pltpu.VMEM((size, cols), jnp.float32),
            pltpu.VMEM((total + 1, depth, size), jnp.bfloat16),
            pltpu.VMEM((depth, size), jnp.float32),
            pltpu.VMEM((size, depth // 2), jnp.float32),
            pltpu.VMEM((depth // 2, depth), jnp.float32),
            pltpu.SMEM((targets,), jnp.int32),
            DMA,
            DMA((2,)),
        ],
        compiler_params=pltpu.CompilerParams(vmem_limit_bytes=LIMIT),
        name="panel",
    )(
        table, got, front, pivots, upper_inverse, lower_inverse, column_basis, row_basis,
        column_ranks, row_ranks,
    )


def spread_kernel(
    n_row, n_col, a_src, b_src, a_all, b_all, a_part_send, a_part_recv, b_part_send, b_part_recv,
    a_send, a_recv, b_send, b_recv, swap_sem, own_sem,
):
    r, c = lax.axis_index("row"), lax.axis_index("col")
    half = n_col // 2
    chip, core = c // 2, lax.rem(c, 2)
    sibling = (r, chip * 2 + 1 - core)
    barrier = pltpu.get_barrier_semaphore()

    def mates(n, me, body):
        def one(k, carry):
            body(lax.rem(me + k, n))
            return carry

        lax.fori_loop(1, n, one, 0)

    mates(n_col, c, lambda o: pl.semaphore_signal(barrier, 1, device_id=(r, o), device_id_type=MESH))
    mates(n_row, r, lambda o: pl.semaphore_signal(barrier, 1, device_id=(o, c), device_id_type=MESH))
    pl.semaphore_wait(barrier, n_col + n_row - 2)

    def piece(o):
        return lax.rem(o, 2) * half + o // 2

    def a_part(o):
        return remote(a_src.at[piece(o)], a_all.at[piece(o)], a_part_send.at[o], a_part_recv, (r, o))

    def b_part(o):
        return remote(b_src.at[o], b_all.at[o], b_part_send.at[o], b_part_recv, (o, c))

    def a_full(h):
        at = piece(c)
        return remote(a_all.at[at], a_all.at[at], a_send.at[h], a_recv.at[chip], (r, h * 2 + core))

    def a_from(h):
        at = core * half + h
        return remote(a_all.at[at], a_all.at[at], a_send.at[h], a_recv.at[h], (r, h * 2 + core))

    def b_full(o):
        return remote(b_all.at[r], b_all.at[r], b_send.at[o], b_recv.at[r], (o, c))

    def b_from(o):
        return remote(b_all.at[o], b_all.at[o], b_send.at[o], b_recv.at[o], (o, c))

    def swap(side):
        part = a_all.at[pl.ds(side * half, half)]
        return remote(part, part, swap_sem.at[0], swap_sem.at[1], sibling)

    @pl.when(c == 0)
    def _():
        mates(n_col, c, lambda o: a_part(o).start())
        own = pltpu.make_async_copy(a_src.at[0], a_all.at[0], own_sem.at[0])
        own.start()
        own.wait()

    @pl.when(r == 0)
    def _():
        mates(n_row, r, lambda o: b_part(o).start())
        own = pltpu.make_async_copy(b_src.at[0], b_all.at[0], own_sem.at[1])
        own.start()
        own.wait()

    @pl.when(c != 0)
    def _():
        a_part(c).wait_recv()

    mates(half, chip, lambda h: a_full(h).start())

    @pl.when(r != 0)
    def _():
        b_part(r).wait_recv()

    mates(n_row, r, lambda o: b_full(o).start())
    mates(half, chip, lambda h: a_from(h).wait_recv())
    swap(core).start()
    mates(n_row, r, lambda o: b_from(o).wait_recv())
    swap(1 - core).wait_recv()
    mates(half, chip, lambda h: a_full(h).wait_send())
    mates(n_row, r, lambda o: b_full(o).wait_send())
    swap(core).wait_send()

    @pl.when(c == 0)
    def _():
        mates(n_col, c, lambda o: a_part(o).wait_send())

    @pl.when(r == 0)
    def _():
        mates(n_row, r, lambda o: b_part(o).wait_send())


def spread(a_src, b_src, n_row, n_col):
    return pl.pallas_call(
        functools.partial(spread_kernel, n_row, n_col),
        out_shape=(
            jax.ShapeDtypeStruct(a_src.shape, a_src.dtype),
            jax.ShapeDtypeStruct(b_src.shape, b_src.dtype),
        ),
        in_specs=[VMEM, VMEM],
        out_specs=(VMEM, VMEM),
        scratch_shapes=[
            DMA((n_col,)), DMA, DMA((n_row,)), DMA,
            DMA((n_col // 2,)), DMA((n_col // 2,)), DMA((n_row,)), DMA((n_row,)), DMA((2,)), DMA((2,)),
        ],
        compiler_params=pltpu.CompilerParams(collective_id=1, has_side_effects=True),
        name="spread",
    )(a_src, b_src)


def finish_kernel(
    total, counts, order, got, front, a_all, b_all, pivots, upper_inverse, lower_inverse, out,
    extended, buffer, b_cat, inverse_parts, corner, base, sem, front_sem, out_sem,
):
    size = upper_inverse.shape[0]
    row_blocks, col_blocks = front.shape[0] // size, front.shape[1] // size
    lanes = a_all.shape[2]
    rank = lanes // 2
    pieces = size // lanes
    is_top, is_left = lax.axis_index("row") == 0, lax.axis_index("col") == 0

    def rows(i):
        return pl.ds(pl.multiple_of(i * size, size), size)

    def load(i):
        return pltpu.make_async_copy(front.at[rows(i)], extended.at[rows(i)], front_sem.at[i])

    def store(i):
        return pltpu.make_async_copy(extended.at[rows(i)], out.at[rows(i)], out_sem.at[i])

    load(0).start()

    def fetch(i, at):
        for j in range(col_blocks):
            at = fetch_target(
                i * col_blocks + j, at, total, counts, order, base, got, buffer, sem.at[i]
            )
        pl.when(i + 1 < row_blocks)(lambda: load(i + 1).start())
        return at

    lax.fori_loop(0, row_blocks, fetch, 0)
    buffer[buffer.shape[0] - 1] = jnp.zeros(buffer.shape[1:], buffer.dtype)

    @pl.when(is_left)
    def _():
        high, low = split(upper_inverse[...])
        inverse_parts[0:size] = high
        inverse_parts[size : 2 * size] = low
        inverse_parts[2 * size :] = high

    for k in range(b_all.shape[0]):
        cols = slice(k * lanes, (k + 1) * lanes)
        high, low = b_all[k, 0:rank, :], b_all[k, rank:, :]
        if k < pieces:
            high = jnp.where(is_left, jnp.zeros_like(high), high)
            low = jnp.where(is_left, jnp.zeros_like(low), low)
        for h in range(2):
            b_cat[h * rank : (h + 1) * rank, cols] = high
            b_cat[(2 + h) * rank : (3 + h) * rank, cols] = low

    def step(i, c):
        load(i).wait()
        for j in range(col_blocks):
            await_target(i * col_blocks + j, counts, got, buffer, sem.at[i])
        a = jnp.concatenate([a_all[i * pieces + k] for k in range(pieces)], axis=0)
        a = jnp.concatenate([a, a], axis=1)
        a = jnp.where(jnp.logical_and(is_top, i == 0), jnp.zeros_like(a), a)
        for j in range(col_blocks):
            cols = slice(j * size, (j + 1) * size)
            added = product(i * col_blocks + j, 0, counts, base, buffer)
            extended[rows(i), cols] += added - dot(a, b_cat[:, cols])
        for j in range(col_blocks):
            cols = slice(j * size, (j + 1) * size)
            add_rest(i * col_blocks + j, counts, base, buffer, extended, rows(i), cols)

        @pl.when(jnp.logical_and(is_left, jnp.logical_not(jnp.logical_and(is_top, i == 0))))
        def _():
            high, low = split(extended[rows(i), 0:size])
            extended[rows(i), 0:size] = dot(
                jnp.concatenate([high, high, low], axis=1), inverse_parts[...]
            )

        @pl.when(jnp.logical_and(is_top, i == 0))
        def _():
            permute = permutation(pivots[...])
            corner[...] = dot(permute, extended[0:size, 0:size], ((0,), (0,)), precision=HIGHEST)
            weights = dot(lower_inverse[...], permute, ((1,), (1,)), precision=HIGHEST)
            for j in range(col_blocks):
                cols = slice(j * size, (j + 1) * size)
                upper = dot(weights, extended[0:size, cols], precision=HIGHEST)
                if j == 0:
                    upper = jnp.where(is_left, corner[...], upper)
                extended[0:size, cols] = upper

        store(i).start()
        return c

    lax.fori_loop(0, row_blocks, step, 0)
    for i in range(row_blocks):
        store(i).wait()


def finish(counts, order, got, front, a_all, b_all, pivots, upper_inverse, lower_inverse, total):
    depth, size = got.shape[1:]
    rows, cols = front.shape
    row_blocks = rows // size
    targets = row_blocks * (cols // size)
    return pl.pallas_call(
        functools.partial(finish_kernel, total),
        out_shape=jax.ShapeDtypeStruct(front.shape, jnp.float32),
        in_specs=[SMEM, SMEM, HBM, HBM, VMEM, VMEM, VMEM, VMEM, VMEM],
        out_specs=HBM,
        scratch_shapes=[
            pltpu.VMEM(front.shape, jnp.float32),
            pltpu.VMEM((total + 1, depth, size), jnp.bfloat16),
            pltpu.VMEM((2 * depth, cols), jnp.bfloat16),
            pltpu.VMEM((3 * size, size), jnp.bfloat16),
            pltpu.VMEM((size, size), jnp.float32),
            pltpu.SMEM((targets,), jnp.int32),
            DMA((row_blocks,)), DMA((row_blocks,)), DMA((row_blocks,)),
        ],
        compiler_params=pltpu.CompilerParams(vmem_limit_bytes=LIMIT),
        name="finish",
    )(counts, order, got, front, a_all, b_all, pivots, upper_inverse, lower_inverse)


def shards(
    front, child_left, child_right, child_owner, child_slot, pivots, upper_inverse, lower_inverse,
    column_basis, row_basis, column_ranks, row_ranks,
):
    n_row, n_col = lax.axis_size("row"), lax.axis_size("col")
    devices = n_row * n_col
    packed, table = pack(
        child_owner[:, 0], child_slot, jnp.swapaxes(child_left, 1, 2), child_right, devices
    )
    got, got_table, relayed = exchange(packed, table, n_row, n_col)
    rounds = (jnp.max(got_table[:, 0, 3]) >= 0).astype(jnp.int32)
    got = lax.fori_loop(0, rounds, lambda i, g: exchange_last(packed, g, n_row, n_col), got)
    got = got.reshape((3 * devices,) + got.shape[2:])
    a_src, b_src, counts, order = panel(
        got_table, got, front, pivots[None, :], upper_inverse, lower_inverse, column_basis.T,
        row_basis.T, column_ranks, row_ranks,
    )
    a_all, b_all = spread(a_src, b_src, n_row, n_col)
    return finish(
        counts, order, got, front, a_all, b_all, pivots[None, :], upper_inverse, lower_inverse,
        devices * CAP,
    )


def solution(mesh):
    in_specs = (
        P("row", "col"),
        P(("row", "col"), None, None),
        P(("row", "col"), None, None),
        P(("row", "col"), None),
        P(("row", "col")),
        P(),
        P(),
        P(),
        P(),
        P(),
        P("row"),
        P("col"),
    )
    out_specs = P("row", "col")
    return jax.shard_map(shards, mesh=mesh, in_specs=in_specs, out_specs=out_specs, check_vma=False)
```

time: 758 us -> 255 us (0.34)
  waiting for transfers between devices: 381 us -> 0 us
  Pallas kernels: 0 us -> 252 us
  other arithmetic: 152 us -> 1.68 us
  local copies, waits for them, and re-layouts: 102 us -> 0 us
  matrix products: 70.8 us -> 0 us
  starting transfers between devices: 33.9 us -> 0 us
  between operations: 13.6 us -> 0.69 us
    pallas_call x0 -> x5, Pallas kernels: none -> 252 us  [the longest x1 187 us: exchange(): pl.pallas_call(functools.partial(exchange_kernel, n_row, n_col), out_shap...]
    psum x2 -> x0, waiting for transfers between devices: 211 us -> none  [from_root(): return lax.psum(kept, axis)]
    all_to_all x3 -> x0, waiting for transfers between devices: 170 us -> none  [the longest x1 85.6 us: shards(): lax.all_to_all(right_buffer.reshape(devices, CAP, rank_width, block_size)...]
    scatter-add x8 -> x0, other arithmetic: 143 us -> none  [apply_group(): front_grid.at[safe_ids // col_blocks, :, safe_ids % col_blocks, :]]
    dot_general x15 -> x0, matrix products: 70.8 us -> none  [the longest x8 49.8 us: apply_group(): jnp.einsum('nbr,nrc->nbc', left_part, right_part, preferred_element_type=...]
    scatter x3 -> x0, local copies, waits for them, and re-layouts: 35 us -> none  [the longest x1 17 us: shards(): jnp.zeros((slot_total, rank_width, block_size), jnp.bfloat16).at[target]]
    all_to_all x3 -> x0, starting transfers between devices: 33.6 us -> none  [the longest x1 13.2 us: shards(): lax.all_to_all(right_buffer.reshape(devices, CAP, rank_width, block_size)...]
    while x2 -> x0, local copies, waits for them, and re-layouts: 18.5 us -> none  [shards(): lax.scan(apply_group, front.reshape(row_blocks, block_size, col_blocks, b...]
  transfers between devices with their start and end apart: 5 -> 0, of which waited for: 4 -> 0; matrix products, arithmetic and copies ran while one was open for 10% -> 0% of each run, Pallas kernels for 0% -> 0%
where the time goes in v1:
time: 255 us; the launch traced here: 254 us
  Pallas kernels  252 us (99%)
    pallas_call x1, Pallas kernels, exchange(): pl.pallas_call(functools.partial(exchange_kernel, n_row, n_col), out_shap...  187 us
    pallas_call x1, Pallas kernels, finish(): pl.pallas_call(functools.partial(finish_kernel, total), out_shape=jax.Sha...  22.9 us
    pallas_call x1, Pallas kernels, spread(): pl.pallas_call(functools.partial(spread_kernel, n_row, n_col), out_shape=...  19 us
    pallas_call x1, Pallas kernels, panel(): pl.pallas_call(functools.partial(panel_kernel, total), out_shape=(jax.Sha...  15.7 us
    pallas_call x1, Pallas kernels, pack(): pl.pallas_call(functools.partial(pack_kernel, devices), out_shape=(jax.Sh...  7.44 us

profile of v1, /device:TPU:32, one launch (start us, length us, event | category | flops | bytes accessed | tf_op | source)
XLA Modules:
  0.0 254.4 jit_solution(5676287945998196263)
XLA Ops:
  0.0 7.4 %pack.1 = (bf16[256,128,256]{2,1,0:T(8,128)(2,1)}, s32[128,1,128]{2,1,0:T(1,128)}) custom-call(s32[112]{0:T(128)} %bitcast.15, s32[1,112]{1,0:T(1,128)} %bitcast.16, s32[1,112]{1,0:T(1,128)} %bitcast.17, bf16[112,64,256]{2,1,0:T(8,128)(2,1)} %bitcast.10, bf16[112,64,256]{2,1,0:T(8,128)(2,1)} %right.1), custom_call_target="tpu_custom_call" | custom-call | tf_op jit(solution)/shard_map/pack/pallas_call | solution.py:108
  7.5 186.9 %exchange.1 = (bf16[3,128,128,256]{3,2,1,0:T(8,128)(2,1)}, s32[128,1,128]{2,1,0:T(1,128)}, bf16[192,128,256]{2,1,0:T(8,128)(2,1)}) custom-call(bf16[256,128,256]{2,1,0:T(8,128)(2,1)} %get-tuple-element.89.packed, s32[128,1,128]{2,1,0:T(1,128)} %get-tuple-element.40.table), custom_call_target="tpu_custom_call" | custom-call | tf_op jit(solution)/shard_map/exchange/pallas_call | solution.py:306
  194.4 1.7 slice_reduce_fusion
  196.7 15.7 %panel.1 = (bf16[16,128,128]{2,1,0:T(8,128)(2,1)}, bf16[8,128,128]{2,1,0:T(8,128)(2,1)}, s32[33]{0:T(128)}, s32[8704]{0:T(1024)}) custom-call(s32[128,1,128]{2,1,0:T(1,128)} %get-tuple-element.41.table, bf16[384,128,256]{2,1,0:T(8,128)(2,1)} %bitcast.8, f32[2048,1024]{1,0:T(8,128)} %front.3, s32[1,256]{1,0:T(1,128)} %bitcast.13, f32[256,256]{1,0:T(8,128)} %upper_inverse.3, ...), custom_call_target="tpu_custom_call" | custom-call | tf_op jit(solution)/shard_map/panel/pallas_call | solution.py:639
  212.5 19.0 %spread.1 = (bf16[16,128,128]{2,1,0:T(8,128)(2,1)}, bf16[8,128,128]{2,1,0:T(8,128)(2,1)}) custom-call(bf16[16,128,128]{2,1,0:T(8,128)(2,1)} %get-tuple-element.46.a_src, bf16[8,128,128]{2,1,0:T(8,128)(2,1)} %get-tuple-element.47.b_src), custom_call_target="tpu_custom_call" | custom-call | tf_op jit(solution)/shard_map/spread/pallas_call | solution.py:759
  231.5 22.9 %finish.1 = f32[2048,1024]{1,0:T(8,128)} custom-call(s32[33]{0:T(128)} %get-tuple-element.44.counts, s32[8704]{0:T(1024)} %get-tuple-element.45.order, bf16[384,128,256]{2,1,0:T(8,128)(2,1)} %bitcast.9, f32[2048,1024]{1,0:T(8,128)} %front.3, bf16[16,128,128]{2,1,0:T(8,128)(2,1)} %get-tuple-element.48.a_all, bf16[8,128,128]{2,1,0:T(8,128)(2,1)} %get-tuple-element.49.b_all, ...), custom_call_target="tpu_custom_call" | custom-call | tf_op jit(solution)/shard_map/finish/pallas_call | solution.py:873
  (1 shorter events, 0.0 us)

commit v2 on v1

--- a/solution.py
+++ b/solution.py
@@ -92,10 +92,13 @@
             o = owner[i]
             p = placed[o]
             placed[o] = 1
-            chip = o // 2
-            late = jnp.logical_and(o % 2 == 1, named[o - o % 2] == 2)
-            extra = jnp.where(late, devices + chips + chip, devices + chip)
-            at = jnp.where(p == 0, o, extra)
+            core = o & 1
+            x, y, z = o >> 5, (o >> 2) & 3, (o & 2) | ((o >> 4) & 1)
+            late = jnp.logical_and(core == 1, named[o - core] == 2)
+            first = jnp.where(core == 0, x * 16 + y * 4 + z, chips + y * 16 + z * 4 + x)
+            second = 2 * chips + z * 16 + x * 4 + y
+            extra = jnp.where(late, 3 * chips + (o >> 1), second)
+            at = jnp.where(p == 0, first, extra)
             pltpu.make_async_copy(staged.at[i], packed.at[at], out_sem).start()
             return c
 
@@ -160,27 +163,60 @@
     )
 
 
+class Ring:
+    def __init__(self, at, go, source, target, relay, send_sem, recv_sem, origin=0):
+        self.at, self.go, self.source, self.target = at, go, source, target
+        self.relay, self.send_sem, self.recv_sem, self.origin = relay, send_sem, recv_sem, origin
+
+    def copy(self, src, dst, i, way):
+        return remote(src, dst, self.send_sem.at[i], self.recv_sem.at[i], self.go(1 if way == 0 else 3))
+
+    def by(self, d):
+        return lax.rem(self.at + d, RING)
+
+    def begin(self):
+        for way in range(2):
+            self.copy(self.source(self.by(2), way), self.relay(way), 4 + way, way).start()
+        for way, d in ((0, 1), (1, 3)):
+            self.copy(self.source(self.by(d), None), self.target(self.at, None), way, way).start()
+
+    def begin_sent(self):
+        for way in range(2):
+            self.copy(self.source(self.by(2), way), self.relay(way), 4 + way, way).wait_send()
+        for way, d in ((0, 1), (1, 3)):
+            self.copy(self.source(self.by(d), None), self.target(self.at, None), way, way).wait_send()
+
+    def forward(self):
+        for way, d in ((0, 3), (1, 1)):
+            held = self.relay(way)
+            self.copy(held, held, 4 + way, way).wait_recv()
+            self.copy(held, self.target(self.by(d), way), 2 + way, way).start()
+
+    def forward_sent(self):
+        for way, d in ((0, 3), (1, 1)):
+            self.copy(self.relay(way), self.target(self.by(d), way), 2 + way, way).wait_send()
+
+    def arrived(self):
+        for way, d in ((0, 3), (1, 1)):
+            part = self.target(self.by(d), None)
+            self.copy(part, part, way, way).wait_recv()
+        for way in range(2):
+            part = self.target(self.by(2), way)
+            self.copy(part, part, 2 + way, way).wait_recv()
+
+
 def exchange_kernel(
-    n_row, n_col, packed, table, got, got_table, relay, table_sems, block_sems, relay_sem,
-    shared_sem, own_sem,
+    n_row, n_col, packed, table, got, got_table, a_one, a_two, t_one, t_two, a_relay_one,
+    a_relay_two, a_relay_three, t_relay_one, t_relay_two, t_relay_three, a_stage_one, a_stage_two,
+    a_stage_three, t_stage, t_last, table_sems, send_sems, recv_sems, hand_sems, own_sems,
 ):
     devices = n_row * n_col
     x, y, z, core = position()
+    here = (x, y, z)
     mine = place_of(x, y, z, core)
     me = mine[0] * n_col + mine[1]
     sibling = place_of(x, y, z, 1 - core)
-    sibling_id = sibling[0] * n_col + sibling[1]
-    chip = me // 2
     barrier = pltpu.get_barrier_semaphore()
-    a_send, a_recv, t_send, r_send, f_send, f_recv = [block_sems.at[i] for i in range(6)]
-
-    own = (
-        pltpu.make_async_copy(packed.at[me], got.at[0, me], own_sem.at[0]),
-        pltpu.make_async_copy(packed.at[devices + chip], got.at[1, me], own_sem.at[1]),
-        pltpu.make_async_copy(table.at[me], got_table.at[me], own_sem.at[2]),
-    )
-    for copy in own:
-        copy.start()
 
     def others(body):
         def one(k, carry):
@@ -190,132 +226,229 @@
 
         lax.fori_loop(1, devices, one, 0)
 
+    own_table = pltpu.make_async_copy(table.at[me], got_table.at[me], own_sems.at[6])
+    own_table.start()
     others(lambda o, at: pl.semaphore_signal(barrier, 1, device_id=at, device_id_type=MESH))
     pl.semaphore_wait(barrier, devices - 1)
 
-    def at_step(steps, core):
-        return place_of(x + steps[0], y + steps[1], z + steps[2], core)
-
-    def number(device):
-        return device[0] * n_col + device[1]
-
-    def kinds(up):
-        return (
-            (0, 0, 1, a_send, lambda d: a_recv),
-            (0, 1, 0, a_send, lambda d: a_recv),
-            (1, core, up, t_send, lambda d: shared_sem.at[d]),
+    def along(axis, to_core):
+        def go(d):
+            return place_of(*[here[i] + (d if i == axis else 0) for i in range(3)], to_core)
+
+        return here[axis], go
+
+    def along_mine(phase):
+        axes = [lax.rem(phase + core, 3) == i for i in range(3)]
+        picked = [axes[i].astype(jnp.int32) for i in range(3)]
+        at = sum(p * h for p, h in zip(picked, here))
+        return at, lambda d: place_of(*[h + d * p for p, h in zip(picked, here)], core)
+
+    def half(ref_at, width):
+        return lambda i, h: ref_at(i, pl.ds(0, 2 * width) if h is None else pl.ds(h * width, width))
+
+    def first_rings(kind):
+        at, go = along(kind, kind)
+        return Ring(
+            at, go, half(lambda j, s: packed.at[kind, j, s], 2),
+            half(lambda i, s: a_one.at[i * 2 + core, s], 2), lambda way: a_relay_one.at[way, core],
+            send_sems.at[kind], recv_sems.at[core],
         )
 
-    def source_block(layer, target):
-        return packed.at[devices + number(target) // 2 if layer else number(target)]
-
-    def first_leg(k):
-        d, steps, far, both, up = step_of(k)
-        for i, (layer, side, way, send, recv) in enumerate(kinds(up)):
-            first, second = legs(steps, far, way)
-            remote(
-                source_block(layer, at_step(steps, side)), relay.at[i * CHIPS + d], send,
-                relay_sem.at[i * CHIPS + d], at_step(first, core),
-            ).start()
-
-    def direct(k):
-        d, steps, far, both, up = step_of(k)
-        for layer, side, way, send, recv in kinds(up):
-            target = at_step(steps, side)
-            remote(source_block(layer, target), got.at[layer, me], send, recv(d), target).start()
-
-    def second_leg(k):
-        d, steps, far, both, up = step_of(k)
-
-        @pl.when(both)
-        def _():
-            for i, (layer, side, way, send, recv) in enumerate(kinds(up)):
-                first, second = legs(steps, far, way)
-                source = number(at_step([4 - f for f in first], core))
-                target = at_step(second, side)
-                held = relay.at[i * CHIPS + d]
-                remote(held, held, r_send, relay_sem.at[i * CHIPS + d], target).wait_recv()
-                remote(held, got.at[layer, source], r_send, recv(d), target).start()
-
-    def hand_over(k):
-        d, steps, far, both, up = step_of(k)
-        source = number(place_of(x + RING - steps[0], y + RING - steps[1], z + RING - steps[2], core))
-        remote(got.at[1, source], got.at[1, source], f_send, shared_sem.at[d], sibling).wait_recv()
-        remote(got.at[1, source], got.at[1, source], f_send, f_recv, sibling).start()
+    def first_mine(origin):
+        at, go = along_mine(0)
+        return Ring(
+            at, go, None, half(lambda i, s: a_one.at[i * 2 + origin, s], 2),
+            lambda way: a_relay_one.at[way, origin], send_sems.at[2 + origin], recv_sems.at[origin],
+        )
+
+    at, go = along_mine(1)
+    a_second = Ring(
+        at, go, half(lambda j, s: a_one.at[s, j], 4), half(lambda i, s: a_two.at[i, s], 4),
+        lambda way: a_relay_two.at[way], send_sems.at[4], recv_sems.at[2],
+    )
+    at, go = along_mine(2)
+    a_third = Ring(
+        at, go, half(lambda j, s: a_two.at[s, slice(None), j], 2), half(lambda i, s: got.at[i, s], 2),
+        lambda way: a_relay_three.at[way], send_sems.at[5], recv_sems.at[3],
+    )
+    t_first = Ring(
+        *along(2, core), half(lambda j, s: packed.at[2, j, s], 2), half(lambda i, s: t_one.at[i, s], 2),
+        lambda way: t_relay_one.at[way], send_sems.at[6], recv_sems.at[4],
+    )
+
+    def t_two_part(i, h):
+        begin = lax.rem(i, 2) * 4
+        part = pl.ds(begin, 4) if h is None else pl.ds(begin + 2 * h, 2)
+        return t_two.at[i // 2, part]
+
+    t_second = Ring(
+        *along(0, core), half(lambda j, s: t_one.at[s, j], 2), t_two_part,
+        lambda way: t_relay_two.at[way], send_sems.at[7], recv_sems.at[5],
+    )
+
+    def t_got(side):
+        def part(i, h):
+            begin = lax.rem(i, 2) * 2
+            rows = pl.ds(begin, 2) if h is None else pl.ds(begin + h, 1)
+            return got.at[4 + side * 2 + i // 2, rows]
+
+        return part
+
+    t_third = Ring(
+        *along(1, core), half(lambda j, s: t_two.at[s, slice(None), j], 1), t_got(core),
+        lambda way: t_relay_three.at[way], send_sems.at[8], recv_sems.at[6],
+    )
+
+    class Keep:
+        def __init__(self, src, stage, dst, i):
+            self.load = pltpu.make_async_copy(src, stage, own_sems.at[i])
+            self.store = pltpu.make_async_copy(stage, dst, own_sems.at[i])
+
+        def run(self):
+            self.load.wait()
+            self.store.start()
+
+    def keep(ring, stage, i):
+        return Keep(ring.source(ring.at, None), stage, ring.target(ring.at, None), i)
+
+    def to_sibling(kind):
+        ring = first_rings(kind)
+        return remote(
+            ring.source(ring.at, None), ring.target(ring.at, None), hand_sems.at[0, 4],
+            hand_sems.at[1, 4], sibling,
+        )
 
     others(
         lambda o, at: remote(
             table.at[o], got_table.at[me], table_sems.at[0], table_sems.at[1], at
         ).start()
     )
-    remote(packed.at[sibling_id], got.at[0, me], a_send, a_recv, sibling).start()
-    remote(packed.at[devices + chip], got.at[1, me], f_send, f_recv, sibling).start()
-    def far_step(k, carry):
-        both = step_of(k)[3]
-
-        @pl.when(both)
-        def _():
-            first_leg(k)
-
-        return carry
-
-    def far_relay(k, carry):
-        far_step(k, carry)
-        second_leg(k - LEAD)
-        return carry
-
-    def relay_only(k, carry):
-        second_leg(k)
-        return carry
-
-    def near_step(k, carry):
-        both = step_of(k)[3]
-        pl.when(jnp.logical_not(both))(lambda: direct(k))
-        return carry
-
-    def end(k, carry):
-        hand_over(k)
-        return carry
-
-    lax.fori_loop(1, LEAD + 1, far_step, 0)
-    lax.fori_loop(LEAD + 1, CHIPS, far_relay, 0)
-    lax.fori_loop(1, CHIPS // 2, near_step, 0)
-    lax.fori_loop(CHIPS - LEAD, CHIPS, relay_only, 0)
-    lax.fori_loop(CHIPS // 2, CHIPS, near_step, 0)
-    lax.fori_loop(1, CHIPS, end, 0)
-    for copy in own:
-        copy.wait()
-
-    def settle(ref, count, sem):
-        part = ref.at[pl.ds(0, count)]
-        pltpu.make_async_copy(part, part, sem).wait()
-
-    settle(got_table, devices - 1, table_sems.at[1])
-    settle(table, devices - 1, table_sems.at[0])
-    settle(got.at[0], devices - 1, a_recv)
-    settle(got.at[1], CHIPS, f_recv)
-    settle(packed, devices - 1, a_send)
-    settle(packed, CHIPS - 1, t_send)
-    settle(relay, 3 * far_count(), r_send)
-    settle(got.at[1], CHIPS, f_send)
+    first_rings(0).begin()
+    first_rings(1).begin()
+    t_first.begin()
+    for kind in range(2):
+        ring = first_rings(kind)
+
+        @pl.when(core == kind)
+        def _():
+            Keep(ring.source(ring.at, None), a_stage_one, ring.target(ring.at, None), 0).load.start()
+
+        @pl.when(core != kind)
+        def _():
+            to_sibling(kind).start()
+
+    t_keep = keep(t_first, t_stage.at[0], 1)
+    t_keep.load.start()
+    for kind in range(2):
+        ring = first_rings(kind)
+
+        @pl.when(core == kind)
+        def _():
+            Keep(ring.source(ring.at, None), a_stage_one, ring.target(ring.at, None), 0).run()
+
+    t_keep.run()
+    for origin in range(2):
+        first_mine(origin).forward()
+    t_first.forward()
+    for origin in range(2):
+        first_mine(origin).arrived()
+    for kind in range(2):
+        ring = first_rings(kind)
+
+        @pl.when(core == kind)
+        def _():
+            Keep(ring.source(ring.at, None), a_stage_one, ring.target(ring.at, None), 0).store.wait()
+
+        @pl.when(core != kind)
+        def _():
+            to_sibling(kind).wait_send()
+
+        @pl.when(core == kind)
+        def _():
+            to_sibling(kind).wait_recv()
+
+    a_second.begin()
+    a_keep = keep(a_second, a_stage_two, 2)
+    a_keep.load.start()
+    t_first.arrived()
+    t_keep.store.wait()
+    t_second.begin()
+    t_keep = keep(t_second, t_stage.at[1], 3)
+    t_keep.load.start()
+    a_keep.run()
+    t_keep.run()
+    a_second.forward()
+    t_second.forward()
+    a_second.arrived()
+    a_keep.store.wait()
+    a_third.begin()
+    a_keep = keep(a_third, a_stage_three, 4)
+    a_keep.load.start()
+    t_second.arrived()
+    t_keep.store.wait()
+    t_third.begin()
+    last = Keep(t_third.source(y, None), t_last, t_third.target(y, None), 5)
+    last.load.start()
+    a_keep.run()
+    last.run()
+    t_third.forward()
+    a_third.forward()
+    last.store.wait()
+
+    def hand(side, d):
+        part = t_got(side)(lax.rem(y + d, RING), None)
+        return remote(part, part, hand_sems.at[0, d], hand_sems.at[1, d], sibling)
+
+    hand(core, 0).start()
+    t_third.arrived()
+    for d in range(1, RING):
+        hand(core, d).start()
+    a_third.arrived()
+    a_keep.store.wait()
+    for d in range(RING):
+        hand(1 - core, d).wait_recv()
+    own_table.wait()
+    first_rings(0).begin_sent()
+    first_rings(1).begin_sent()
+    for origin in range(2):
+        first_mine(origin).forward_sent()
+    for ring in (t_first, a_second, t_second, a_third, t_third):
+        ring.begin_sent()
+        ring.forward_sent()
+    for d in range(RING):
+        hand(core, d).wait_send()
+    rest = pl.ds(0, devices - 1)
+    pltpu.make_async_copy(table.at[rest], got_table.at[rest], table_sems.at[1]).wait()
+    pltpu.make_async_copy(table.at[rest], got_table.at[rest], table_sems.at[0]).wait()
 
 
 def exchange(packed, table, n_row, n_col):
-    devices = n_row * n_col
-    block = packed.shape[1:]
+    block = packed.shape[4:]
+
+    def held(*shape):
+        return jax.ShapeDtypeStruct(shape + block, packed.dtype)
+
+    def stage(*shape):
+        return pltpu.VMEM(shape + block, packed.dtype)
+
     return pl.pallas_call(
         functools.partial(exchange_kernel, n_row, n_col),
         out_shape=(
-            jax.ShapeDtypeStruct((3, devices) + block, packed.dtype),
-            jax.ShapeDtypeStruct(table.shape, table.dtype),
-            jax.ShapeDtypeStruct((3 * CHIPS,) + block, packed.dtype),
+            held(12, 4, 8), jax.ShapeDtypeStruct(table.shape, table.dtype),
+            held(8, 4, 4), held(4, 8, 4), held(4, 4, 4), held(2, 8, 4),
+            held(2, 2, 2, 4), held(2, 4, 4), held(2, 2, 8), held(2, 2, 4), held(2, 2, 4), held(2, 1, 8),
         ),
         in_specs=[HBM, HBM],
-        out_specs=(HBM, HBM, HBM),
-        scratch_shapes=[DMA((2,)), DMA((6,)), DMA((3 * CHIPS,)), DMA((CHIPS,)), DMA((3,))],
-        compiler_params=pltpu.CompilerParams(collective_id=2, has_side_effects=True),
+        out_specs=(HBM,) * 12,
+        scratch_shapes=[
+            stage(4, 4), stage(8, 4), stage(4, 8), stage(2, 4, 4), stage(2, 8),
+            DMA((2,)), DMA((9, 6)), DMA((7, 6)), DMA((2, 5)), DMA((7,)),
+        ],
+        compiler_params=pltpu.CompilerParams(
+            collective_id=2, has_side_effects=True, vmem_limit_bytes=LIMIT
+        ),
         name="exchange",
-    )(packed, table)
+    )(packed, table)[:2]
 
 
 def last_kernel(n_row, n_col, packed, got_in, got, relay, sems, relay_sem, own_sem):
@@ -323,7 +456,6 @@
     x, y, z, core = position()
     mine = place_of(x, y, z, core)
     me = mine[0] * n_col + mine[1]
-    first_block = devices + CHIPS
     barrier = pltpu.get_barrier_semaphore()
 
     def at_step(steps, core):
@@ -368,7 +500,11 @@
         pl.semaphore_wait(barrier, 26 + 13 + 1)
 
     def block_for(target):
-        return packed.at[first_block + number(target) // 2]
+        chip = number(target) // 2
+        return packed.at[3, chip // 16, lax.rem(chip // 4, 4), lax.rem(chip, 4)]
+
+    def landing(source):
+        return got.at[8 + source // 32, lax.rem(source // 8, 4), lax.rem(source, 8)]
 
     def first_leg(k, carry):
         d, steps, far, both, up = step_of(k)
@@ -389,7 +525,7 @@
         @pl.when(jnp.logical_not(both))
         def _():
             target = at_step(steps, 1)
-            remote(block_for(target), got.at[2, me], sems.at[0], sems.at[1], target).start()
+            remote(block_for(target), landing(me), sems.at[0], sems.at[1], target).start()
 
         return carry
 
@@ -403,7 +539,7 @@
             target = at_step(second, 1)
             held = relay.at[d]
             remote(held, held, sems.at[2], relay_sem.at[d], target).wait_recv()
-            remote(held, got.at[2, source], sems.at[2], sems.at[1], target).start()
+            remote(held, landing(source), sems.at[2], sems.at[1], target).start()
 
         return carry
 
@@ -420,16 +556,16 @@
     @pl.when(core == 0)
     def _():
         to = place_of(x, y, z, 1)
-        remote(packed.at[first_block + me // 2], got.at[2, me], sems.at[0], sems.at[1], to).start()
-        settle(packed, CHIPS, sems.at[0])
+        remote(block_for(to), landing(me), sems.at[0], sems.at[1], to).start()
+        settle(relay, CHIPS, sems.at[0])
 
     @pl.when(core == 1)
     def _():
-        own = pltpu.make_async_copy(packed.at[first_block + me // 2], got.at[2, me], own_sem)
+        own = pltpu.make_async_copy(block_for(mine), landing(me), own_sem)
         own.start()
         own.wait()
-        settle(packed, CHIPS - 1, sems.at[0])
-        settle(got.at[2], devices - 1, sems.at[1])
+        settle(relay, CHIPS - 1, sems.at[0])
+        settle(relay, devices - 1, sems.at[1])
 
 
 def exchange_last(packed, got, n_row, n_col):
@@ -437,7 +573,7 @@
         functools.partial(last_kernel, n_row, n_col),
         out_shape=(
             jax.ShapeDtypeStruct(got.shape, got.dtype),
-            jax.ShapeDtypeStruct((CHIPS,) + packed.shape[1:], packed.dtype),
+            jax.ShapeDtypeStruct((2 * CHIPS,) + packed.shape[4:], packed.dtype),
         ),
         in_specs=[HBM, HBM],
         out_specs=(HBM, HBM),
@@ -515,23 +651,31 @@
     for t in range(targets + 1):
         counts[t] = 0
 
-    def note(s, p):
+    def note(s, p, at):
         t = table[s, 0, p]
         t = jnp.where(t < 0, targets, t)
         n = counts[t]
-        order[t * total + n] = p * devices + s
+        order[t * total + n] = at
         counts[t] = n + 1
 
-    def tally(s, flags):
-        note(s, 0)
-        note(s, 1)
-        return jnp.maximum(flags, table[s, 0, 3])
+    core = lax.rem(lax.axis_index("col"), 2)
+    wx, wy, wz = 2 + core * 30, 8 - core * 6, 32 - core * 24
+
+    def tally(r, flags):
+        x, low = r // 2, lax.rem(r, 2)
+        for q in range(devices // 8):
+            s = r * (devices // 8) + q
+            y, z, c = q // 4, (q // 2) % 2 * 2 + low, q % 2
+            note(s, 0, x * wx + y * wy + z * wz + c)
+            note(s, 1, devices + c * CHIPS + y * 16 + x * 4 + z)
+            flags = jnp.maximum(flags, table[s, 0, 3])
+        return flags
 
     def tally_last(s, c):
-        note(s, 2)
+        note(s, 2, 2 * devices + s)
         return c
 
-    flags = lax.fori_loop(0, devices, tally, -1, unroll=4)
+    flags = lax.fori_loop(0, 8, tally, -1)
     lax.fori_loop(0, jnp.where(flags >= 0, devices, 0), tally_last, 0)
 
     @pl.when(jnp.logical_or(is_top, is_left))
@@ -898,10 +1042,11 @@
     packed, table = pack(
         child_owner[:, 0], child_slot, jnp.swapaxes(child_left, 1, 2), child_right, devices
     )
-    got, got_table, relayed = exchange(packed, table, n_row, n_col)
+    packed = packed.reshape((4, RING, RING, RING) + packed.shape[1:])
+    got, got_table = exchange(packed, table, n_row, n_col)
     rounds = (jnp.max(got_table[:, 0, 3]) >= 0).astype(jnp.int32)
     got = lax.fori_loop(0, rounds, lambda i, g: exchange_last(packed, g, n_row, n_col), got)
-    got = got.reshape((3 * devices,) + got.shape[2:])
+    got = got.reshape((3 * devices,) + got.shape[3:])
     a_src, b_src, counts, order = panel(
         got_table, got, front, pivots[None, :], upper_inverse, lower_inverse, column_basis.T,
         row_basis.T, column_ranks, row_ranks,

time: 255 us -> 227 us (0.89)
  the two profiles are of different devices: /device:TPU:32 before, /device:TPU:8 now
where the time goes in v2:
time: 227 us; the launch traced here: 226 us
  Pallas kernels  224 us (99%)
    pallas_call x1, Pallas kernels, exchange(): pl.pallas_call(functools.partial(exchange_kernel, n_row, n_col), out_shap...  161 us
    pallas_call x1, Pallas kernels, spread(): pl.pallas_call(functools.partial(spread_kernel, n_row, n_col), out_shape=...  25 us
    pallas_call x1, Pallas kernels, finish(): pl.pallas_call(functools.partial(finish_kernel, total), out_shape=jax.Sha...  22.1 us
    pallas_call x1, Pallas kernels, panel(): pl.pallas_call(functools.partial(panel_kernel, total), out_shape=(jax.Sha...  8.16 us
    pallas_call x1, Pallas kernels, pack(): pl.pallas_call(functools.partial(pack_kernel, devices), out_shape=(jax.Sh...  7.5 us

profile of v2, /device:TPU:8, one launch (start us, length us, event | category | flops | bytes accessed | tf_op | source)
XLA Modules:
  0.0 226.5 jit_solution(6524339483000305099)
XLA Ops:
  0.0 7.5 %pack.1 = (bf16[256,128,256]{2,1,0:T(8,128)(2,1)}, s32[128,1,128]{2,1,0:T(1,128)}) custom-call(s32[112]{0:T(128)} %bitcast.18, s32[1,112]{1,0:T(1,128)} %bitcast.19, s32[1,112]{1,0:T(1,128)} %bitcast.20, bf16[112,64,256]{2,1,0:T(8,128)(2,1)} %bitcast.13, bf16[112,64,256]{2,1,0:T(8,128)(2,1)} %right.1), custom_call_target="tpu_custom_call" | custom-call | tf_op jit(solution)/shard_map/pack/pallas_call | solution.py:111
  7.5 161.3 %exchange.1 = (bf16[12,4,8,128,256]{4,3,2,1,0:T(8,128)(2,1)}, s32[128,1,128]{2,1,0:T(1,128)}, bf16[8,4,4,128,256]{4,3,2,1,0:T(8,128)(2,1)}, bf16[4,8,4,128,256]{...) custom-call(bf16[4,4,4,4,128,256]{5,4,3,2,1,0:T(8,128)(2,1)} %bitcas, ...), custom_call_target="tpu_custom_call" | custom-call | tf_op jit(solution)/shard_map/exchange/pallas_call | solution.py:434
  168.8 1.7 slice_reduce_fusion
  171.2 8.2 %panel.1 = (bf16[16,128,128]{2,1,0:T(8,128)(2,1)}, bf16[8,128,128]{2,1,0:T(8,128)(2,1)}, s32[33]{0:T(128)}, s32[8704]{0:T(1024)}) custom-call(s32[128,1,128]{2,1,0:T(1,128)} %get-tuple-element.41.table, bf16[384,128,256]{2,1,0:T(8,128)(2,1)} %bitcast.9, f32[2048,1024]{1,0:T(8,128)} %front.3, s32[1,256]{1,0:T(1,128)} %bitcast.16, f32[256,256]{1,0:T(8,128)} %upper_inverse.3, ...), custom_call_target="tpu_custom_call" | custom-call | tf_op jit(solution)/shard_map/panel/pallas_call | solution.py:783
  179.3 25.0 %spread.1 = (bf16[16,128,128]{2,1,0:T(8,128)(2,1)}, bf16[8,128,128]{2,1,0:T(8,128)(2,1)}) custom-call(bf16[16,128,128]{2,1,0:T(8,128)(2,1)} %get-tuple-element.46.a_src, bf16[8,128,128]{2,1,0:T(8,128)(2,1)} %get-tuple-element.47.b_src), custom_call_target="tpu_custom_call" | custom-call | tf_op jit(solution)/shard_map/spread/pallas_call | solution.py:903
  204.4 22.1 %finish.1 = f32[2048,1024]{1,0:T(8,128)} custom-call(s32[33]{0:T(128)} %get-tuple-element.44.counts, s32[8704]{0:T(1024)} %get-tuple-element.45.order, bf16[384,128,256]{2,1,0:T(8,128)(2,1)} %bitcast.10, f32[2048,1024]{1,0:T(8,128)} %front.3, bf16[16,128,128]{2,1,0:T(8,128)(2,1)} %get-tuple-element.48.a_all, bf16[8,128,128]{2,1,0:T(8,128)(2,1)} %get-tuple-element.49.b_all, ...), custom_call_target="tpu_custom_call" | custom-call | tf_op jit(solution)/shard_map/finish/pallas_call | solution.py:1017
  (1 shorter events, 0.0 us)

commit v3 on v2

--- a/solution.py
+++ b/solution.py
@@ -63,7 +63,11 @@
 
     shape = (devices, 1, count)
     place = lax.broadcasted_iota(jnp.int32, shape, 2)
-    device = lax.broadcasted_iota(jnp.int32, shape, 0)
+    line = lax.broadcasted_iota(jnp.int32, shape, 0)
+    core = line >> 6
+    high, middle, low = (line >> 4) & 3, (line >> 2) & 3, line & 3
+    x, y, z = (jnp.where(core == 0, a, b) for a, b in ((high, low), (middle, high), (low, middle)))
+    device = x * 32 + (z & 1) * 16 + y * 4 + (z & 2) + core
     owners = owner_row[...][None]
     code = (place * 64 + slot_row[...][None]).astype(jnp.float32)
 
@@ -74,7 +78,7 @@
 
     least, most = ends(owners == device)
     low_least, low_most = ends(owners == device - (device & 1))
-    core = device[:, :, 0:1] & 1
+    core = core[:, :, 0:1]
     first = jnp.where(most >= 0.0, least.astype(jnp.int32) & 63, -1)
     second = jnp.where(most > least, most.astype(jnp.int32) & 63, -1)
     late = jnp.logical_and(core == 1, low_most > low_least)
@@ -163,6 +167,18 @@
     )
 
 
+class Together:
+    def __init__(self, *rings):
+        self.rings = rings
+
+    def __getattr__(self, name):
+        def each():
+            for ring in self.rings:
+                getattr(ring, name)()
+
+        return each
+
+
 class Ring:
     def __init__(self, at, go, source, target, relay, send_sem, recv_sem, origin=0):
         self.at, self.go, self.source, self.target = at, go, source, target
@@ -206,30 +222,25 @@
 
 
 def exchange_kernel(
-    n_row, n_col, packed, table, got, got_table, a_one, a_two, t_one, t_two, a_relay_one,
-    a_relay_two, a_relay_three, t_relay_one, t_relay_two, t_relay_three, a_stage_one, a_stage_two,
-    a_stage_three, t_stage, t_last, table_sems, send_sems, recv_sems, hand_sems, own_sems,
+    n_col, packed, table, got, got_table, a_one, a_two, t_one, t_two, a_relay_one,
+    a_relay_two, a_relay_three, t_relay_one, t_relay_two, t_relay_three, l_one, l_two, l_relay_one,
+    l_relay_two, l_relay_three, a_stage_one, a_stage_two, a_stage_three, t_stage, t_last, send_sems,
+    recv_sems, hand_sems, own_sems,
 ):
-    devices = n_row * n_col
     x, y, z, core = position()
     here = (x, y, z)
-    mine = place_of(x, y, z, core)
-    me = mine[0] * n_col + mine[1]
     sibling = place_of(x, y, z, 1 - core)
     barrier = pltpu.get_barrier_semaphore()
 
-    def others(body):
-        def one(k, carry):
-            o = lax.rem(me + k, devices)
-            body(o, (o // n_col, lax.rem(o, n_col)))
-            return carry
-
-        lax.fori_loop(1, devices, one, 0)
-
-    own_table = pltpu.make_async_copy(table.at[me], got_table.at[me], own_sems.at[6])
-    own_table.start()
-    others(lambda o, at: pl.semaphore_signal(barrier, 1, device_id=at, device_id_type=MESH))
-    pl.semaphore_wait(barrier, devices - 1)
+    def greet(at):
+        pl.semaphore_signal(barrier, 1, device_id=at, device_id_type=MESH)
+
+    greet(sibling)
+    for axis in range(3):
+        for d in (1, 3):
+            for side in range(2):
+                greet(place_of(*[here[i] + (d if i == axis else 0) for i in range(3)], side))
+    pl.semaphore_wait(barrier, 13)
 
     def along(axis, to_core):
         def go(d):
@@ -246,31 +257,51 @@
     def half(ref_at, width):
         return lambda i, h: ref_at(i, pl.ds(0, 2 * width) if h is None else pl.ds(h * width, width))
 
-    def first_rings(kind):
+    arrays = (
+        (packed, got, a_one, a_two, a_relay_one, a_relay_two, a_relay_three, 0, 0),
+        (table, got_table, l_one, l_two, l_relay_one, l_relay_two, l_relay_three, 9, 7),
+    )
+
+    def first_ring(kind, which):
+        src, end, one, two, relay, relay_two, relay_three, sent, received = arrays[which]
         at, go = along(kind, kind)
         return Ring(
-            at, go, half(lambda j, s: packed.at[kind, j, s], 2),
-            half(lambda i, s: a_one.at[i * 2 + core, s], 2), lambda way: a_relay_one.at[way, core],
-            send_sems.at[kind], recv_sems.at[core],
+            at, go, half(lambda j, s: src.at[kind, j, s], 2),
+            half(lambda i, s: one.at[i * 2 + core, s], 2), lambda way: relay.at[way, core],
+            send_sems.at[sent + kind], recv_sems.at[received + core],
         )
+
+    def first_rings(kind):
+        return Together(first_ring(kind, 1), first_ring(kind, 0))
 
     def first_mine(origin):
         at, go = along_mine(0)
+
+        def ring(src, end, one, two, relay, relay_two, relay_three, sent, received):
+            return Ring(
+                at, go, None, half(lambda i, s: one.at[i * 2 + origin, s], 2),
+                lambda way: relay.at[way, origin], send_sems.at[sent + 2 + origin],
+                recv_sems.at[received + origin],
+            )
+
+        return Together(ring(*arrays[1]), ring(*arrays[0]))
+
+    def second_ring(which):
+        src, end, one, two, relay, relay_two, relay_three, sent, received = arrays[which]
         return Ring(
-            at, go, None, half(lambda i, s: a_one.at[i * 2 + origin, s], 2),
-            lambda way: a_relay_one.at[way, origin], send_sems.at[2 + origin], recv_sems.at[origin],
+            *along_mine(1), half(lambda j, s: one.at[s, j], 4), half(lambda i, s: two.at[i, s], 4),
+            lambda way: relay_two.at[way], send_sems.at[sent + 4], recv_sems.at[received + 2],
         )
 
-    at, go = along_mine(1)
-    a_second = Ring(
-        at, go, half(lambda j, s: a_one.at[s, j], 4), half(lambda i, s: a_two.at[i, s], 4),
-        lambda way: a_relay_two.at[way], send_sems.at[4], recv_sems.at[2],
-    )
-    at, go = along_mine(2)
-    a_third = Ring(
-        at, go, half(lambda j, s: a_two.at[s, slice(None), j], 2), half(lambda i, s: got.at[i, s], 2),
-        lambda way: a_relay_three.at[way], send_sems.at[5], recv_sems.at[3],
-    )
+    def third_ring(which):
+        src, end, one, two, relay, relay_two, relay_three, sent, received = arrays[which]
+        return Ring(
+            *along_mine(2), half(lambda j, s: two.at[s, slice(None), j], 2),
+            half(lambda i, s: end.at[i, s], 2), lambda way: relay_three.at[way],
+            send_sems.at[sent + 5], recv_sems.at[received + 3],
+        )
+
+    a_second, a_third = Together(second_ring(1), second_ring(0)), Together(third_ring(1), third_ring(0))
     t_first = Ring(
         *along(2, core), half(lambda j, s: packed.at[2, j, s], 2), half(lambda i, s: t_one.at[i, s], 2),
         lambda way: t_relay_one.at[way], send_sems.at[6], recv_sems.at[4],
@@ -311,40 +342,40 @@
     def keep(ring, stage, i):
         return Keep(ring.source(ring.at, None), stage, ring.target(ring.at, None), i)
 
-    def to_sibling(kind):
-        ring = first_rings(kind)
+    def keep_line(ring):
+        return pltpu.make_async_copy(
+            ring.source(ring.at, None), ring.target(ring.at, None), own_sems.at[6]
+        )
+
+    def to_sibling(kind, which):
+        ring = first_ring(kind, which)
         return remote(
-            ring.source(ring.at, None), ring.target(ring.at, None), hand_sems.at[0, 4],
-            hand_sems.at[1, 4], sibling,
+            ring.source(ring.at, None), ring.target(ring.at, None), hand_sems.at[0, 4 + which],
+            hand_sems.at[1, 4 + which], sibling,
         )
 
-    others(
-        lambda o, at: remote(
-            table.at[o], got_table.at[me], table_sems.at[0], table_sems.at[1], at
-        ).start()
-    )
     first_rings(0).begin()
     first_rings(1).begin()
     t_first.begin()
     for kind in range(2):
-        ring = first_rings(kind)
 
         @pl.when(core == kind)
         def _():
-            Keep(ring.source(ring.at, None), a_stage_one, ring.target(ring.at, None), 0).load.start()
+            keep_line(first_ring(kind, 1)).start()
+            keep(first_ring(kind, 0), a_stage_one, 0).load.start()
 
         @pl.when(core != kind)
         def _():
-            to_sibling(kind).start()
+            to_sibling(kind, 1).start()
+            to_sibling(kind, 0).start()
 
     t_keep = keep(t_first, t_stage.at[0], 1)
     t_keep.load.start()
     for kind in range(2):
-        ring = first_rings(kind)
 
         @pl.when(core == kind)
         def _():
-            Keep(ring.source(ring.at, None), a_stage_one, ring.target(ring.at, None), 0).run()
+            keep(first_ring(kind, 0), a_stage_one, 0).run()
 
     t_keep.run()
     for origin in range(2):
@@ -353,23 +384,23 @@
     for origin in range(2):
         first_mine(origin).arrived()
     for kind in range(2):
-        ring = first_rings(kind)
 
         @pl.when(core == kind)
         def _():
-            Keep(ring.source(ring.at, None), a_stage_one, ring.target(ring.at, None), 0).store.wait()
+            keep(first_ring(kind, 0), a_stage_one, 0).store.wait()
+            keep_line(first_ring(kind, 1)).wait()
+            to_sibling(kind, 1).wait_recv()
+            to_sibling(kind, 0).wait_recv()
 
         @pl.when(core != kind)
         def _():
-            to_sibling(kind).wait_send()
-
-        @pl.when(core == kind)
-        def _():
-            to_sibling(kind).wait_recv()
+            to_sibling(kind, 1).wait_send()
+            to_sibling(kind, 0).wait_send()
 
     a_second.begin()
-    a_keep = keep(a_second, a_stage_two, 2)
+    a_keep, line_keep = keep(second_ring(0), a_stage_two, 2), keep_line(second_ring(1))
     a_keep.load.start()
+    line_keep.start()
     t_first.arrived()
     t_keep.store.wait()
     t_second.begin()
@@ -381,9 +412,11 @@
     t_second.forward()
     a_second.arrived()
     a_keep.store.wait()
+    line_keep.wait()
     a_third.begin()
-    a_keep = keep(a_third, a_stage_three, 4)
+    a_keep, line_keep = keep(third_ring(0), a_stage_three, 4), keep_line(third_ring(1))
     a_keep.load.start()
+    line_keep.start()
     t_second.arrived()
     t_keep.store.wait()
     t_third.begin()
@@ -405,9 +438,9 @@
         hand(core, d).start()
     a_third.arrived()
     a_keep.store.wait()
+    line_keep.wait()
     for d in range(RING):
         hand(1 - core, d).wait_recv()
-    own_table.wait()
     first_rings(0).begin_sent()
     first_rings(1).begin_sent()
     for origin in range(2):
@@ -417,32 +450,34 @@
         ring.forward_sent()
     for d in range(RING):
         hand(core, d).wait_send()
-    rest = pl.ds(0, devices - 1)
-    pltpu.make_async_copy(table.at[rest], got_table.at[rest], table_sems.at[1]).wait()
-    pltpu.make_async_copy(table.at[rest], got_table.at[rest], table_sems.at[0]).wait()
-
-
-def exchange(packed, table, n_row, n_col):
-    block = packed.shape[4:]
+
+
+def exchange(packed, table, n_col):
+    block, line = packed.shape[4:], table.shape[4:]
 
     def held(*shape):
         return jax.ShapeDtypeStruct(shape + block, packed.dtype)
 
+    def lines(*shape):
+        return jax.ShapeDtypeStruct(shape + line, table.dtype)
+
     def stage(*shape):
         return pltpu.VMEM(shape + block, packed.dtype)
 
+    out_shape = (
+        held(12, 4, 8), lines(4, 4, 8),
+        held(8, 4, 4), held(4, 8, 4), held(4, 4, 4), held(2, 8, 4),
+        held(2, 2, 2, 4), held(2, 4, 4), held(2, 2, 8), held(2, 2, 4), held(2, 2, 4), held(2, 1, 8),
+        lines(8, 4, 4), lines(4, 8, 4), lines(2, 2, 2, 4), lines(2, 4, 4), lines(2, 2, 8),
+    )
     return pl.pallas_call(
-        functools.partial(exchange_kernel, n_row, n_col),
-        out_shape=(
-            held(12, 4, 8), jax.ShapeDtypeStruct(table.shape, table.dtype),
-            held(8, 4, 4), held(4, 8, 4), held(4, 4, 4), held(2, 8, 4),
-            held(2, 2, 2, 4), held(2, 4, 4), held(2, 2, 8), held(2, 2, 4), held(2, 2, 4), held(2, 1, 8),
-        ),
+        functools.partial(exchange_kernel, n_col),
+        out_shape=out_shape,
         in_specs=[HBM, HBM],
-        out_specs=(HBM,) * 12,
+        out_specs=(HBM,) * len(out_shape),
         scratch_shapes=[
             stage(4, 4), stage(8, 4), stage(4, 8), stage(2, 4, 4), stage(2, 8),
-            DMA((2,)), DMA((9, 6)), DMA((7, 6)), DMA((2, 5)), DMA((7,)),
+            DMA((15, 6)), DMA((11, 6)), DMA((2, 6)), DMA((7,)),
         ],
         compiler_params=pltpu.CompilerParams(
             collective_id=2, has_side_effects=True, vmem_limit_bytes=LIMIT
@@ -634,7 +669,7 @@
 
 
 def panel_kernel(
-    total, table, got, front, pivots, upper_inverse, lower_inverse, column_basis, row_basis,
+    total, table, most, got, front, pivots, upper_inverse, lower_inverse, column_basis, row_basis,
     column_ranks, row_ranks, a_out, b_out, counts, order, left_sum, top_sum, buffer, top_weights,
     left_weights, coupling, base, sem, front_sem,
 ):
@@ -659,24 +694,29 @@
         counts[t] = n + 1
 
     core = lax.rem(lax.axis_index("col"), 2)
-    wx, wy, wz = 2 + core * 30, 8 - core * 6, 32 - core * 24
-
-    def tally(r, flags):
-        x, low = r // 2, lax.rem(r, 2)
-        for q in range(devices // 8):
-            s = r * (devices // 8) + q
-            y, z, c = q // 4, (q // 2) % 2 * 2 + low, q % 2
-            note(s, 0, x * wx + y * wy + z * wz + c)
-            note(s, 1, devices + c * CHIPS + y * 16 + x * 4 + z)
-            flags = jnp.maximum(flags, table[s, 0, 3])
-        return flags
-
-    def tally_last(s, c):
-        note(s, 2, 2 * devices + s)
+    w_high, w_middle, w_low = 1 + core * 3, 16 - core * 15, 4 + core * 12
+
+    def digits(k):
+        return k // 32, lax.rem(k // 8, 4), lax.rem(k // 2, 4), lax.rem(k, 2)
+
+    def tally(k, c):
+        note(k, 0, k)
         return c
 
-    flags = lax.fori_loop(0, 8, tally, -1)
-    lax.fori_loop(0, jnp.where(flags >= 0, devices, 0), tally_last, 0)
+    def tally_shared(k, c):
+        high, middle, low, side = digits(k)
+        note(k, 1, devices + side * CHIPS + high * w_high + middle * w_middle + low * w_low)
+        return c
+
+    def tally_last(k, c):
+        high, middle, low, side = digits(k)
+        x, y, z = (jnp.where(core == 0, a, b) for a, b in ((low, high), (middle, low), (high, middle)))
+        note(k, 2, 2 * devices + x * 32 + lax.rem(z, 2) * 16 + y * 4 + (z // 2) * 2 + side)
+        return c
+
+    lax.fori_loop(0, devices, tally, 0, unroll=8)
+    lax.fori_loop(0, jnp.where(most[1] >= 0, devices, 0), tally_shared, 0)
+    lax.fori_loop(0, jnp.where(most[2] >= 0, devices, 0), tally_last, 0)
 
     @pl.when(jnp.logical_or(is_top, is_left))
     def _():
@@ -773,7 +813,7 @@
 
 
 def panel(
-    table, got, front, pivots, upper_inverse, lower_inverse, column_basis, row_basis, column_ranks,
+    table, most, got, front, pivots, upper_inverse, lower_inverse, column_basis, row_basis, column_ranks,
     row_ranks,
 ):
     depth, size = got.shape[1:]
@@ -788,7 +828,7 @@
             jax.ShapeDtypeStruct((targets + 1,), jnp.int32),
             jax.ShapeDtypeStruct(((targets + 2) * total,), jnp.int32),
         ),
-        in_specs=[SMEM, HBM, HBM, VMEM, VMEM, VMEM, VMEM, VMEM, SMEM, SMEM],
+        in_specs=[SMEM, SMEM, HBM, HBM, VMEM, VMEM, VMEM, VMEM, VMEM, SMEM, SMEM],
         out_specs=(VMEM, VMEM, SMEM, SMEM),
         scratch_shapes=[
             pltpu.VMEM((rows, size), jnp.float32),
@@ -804,7 +844,7 @@
         compiler_params=pltpu.CompilerParams(vmem_limit_bytes=LIMIT),
         name="panel",
     )(
-        table, got, front, pivots, upper_inverse, lower_inverse, column_basis, row_basis,
+        table, most, got, front, pivots, upper_inverse, lower_inverse, column_basis, row_basis,
         column_ranks, row_ranks,
     )
 
@@ -857,30 +897,24 @@
         part = a_all.at[pl.ds(side * half, half)]
         return remote(part, part, swap_sem.at[0], swap_sem.at[1], sibling)
 
+    own_a = pltpu.make_async_copy(a_src.at[0], a_all.at[0], own_sem.at[0])
+    own_b = pltpu.make_async_copy(b_src.at[0], b_all.at[0], own_sem.at[1])
+
     @pl.when(c == 0)
     def _():
+        own_a.start()
         mates(n_col, c, lambda o: a_part(o).start())
-        own = pltpu.make_async_copy(a_src.at[0], a_all.at[0], own_sem.at[0])
-        own.start()
-        own.wait()
 
     @pl.when(r == 0)
     def _():
+        own_b.start()
         mates(n_row, r, lambda o: b_part(o).start())
-        own = pltpu.make_async_copy(b_src.at[0], b_all.at[0], own_sem.at[1])
-        own.start()
-        own.wait()
-
-    @pl.when(c != 0)
-    def _():
-        a_part(c).wait_recv()
-
+
+    pl.when(c == 0)(own_a.wait)
+    pl.when(c != 0)(lambda: a_part(c).wait_recv())
     mates(half, chip, lambda h: a_full(h).start())
-
-    @pl.when(r != 0)
-    def _():
-        b_part(r).wait_recv()
-
+    pl.when(r == 0)(own_b.wait)
+    pl.when(r != 0)(lambda: b_part(r).wait_recv())
     mates(n_row, r, lambda o: b_full(o).start())
     mates(half, chip, lambda h: a_from(h).wait_recv())
     swap(core).start()
@@ -906,8 +940,8 @@
             jax.ShapeDtypeStruct(a_src.shape, a_src.dtype),
             jax.ShapeDtypeStruct(b_src.shape, b_src.dtype),
         ),
-        in_specs=[VMEM, VMEM],
-        out_specs=(VMEM, VMEM),
+        in_specs=[HBM, HBM],
+        out_specs=(HBM, HBM),
         scratch_shapes=[
             DMA((n_col,)), DMA, DMA((n_row,)), DMA,
             DMA((n_col // 2,)), DMA((n_col // 2,)), DMA((n_row,)), DMA((n_row,)), DMA((2,)), DMA((2,)),
@@ -918,14 +952,16 @@
 
 
 def finish_kernel(
-    total, counts, order, got, front, a_all, b_all, pivots, upper_inverse, lower_inverse, out,
-    extended, buffer, b_cat, inverse_parts, corner, base, sem, front_sem, out_sem,
+    total, counts, order, most, got, front, a_in, b_in, pivots, upper_inverse, lower_inverse, out,
+    extended, buffer, a_all, b_all, b_cat, inverse_parts, corner, got_sem, factor_sem, front_sem,
+    out_sem,
 ):
     size = upper_inverse.shape[0]
     row_blocks, col_blocks = front.shape[0] // size, front.shape[1] // size
     lanes = a_all.shape[2]
     rank = lanes // 2
     pieces = size // lanes
+    devices = total // CAP
     is_top, is_left = lax.axis_index("row") == 0, lax.axis_index("col") == 0
 
     def rows(i):
@@ -937,17 +973,25 @@
     def store(i):
         return pltpu.make_async_copy(extended.at[rows(i)], out.at[rows(i)], out_sem.at[i])
 
+    def fetch(layer):
+        part = pl.ds(layer * devices, devices)
+        return pltpu.make_async_copy(got.at[part], buffer.at[part], got_sem.at[layer])
+
+    def fetch_all(act):
+        act(fetch(0))
+        for layer in range(1, 3):
+            pl.when(most[layer] >= 0)(lambda: act(fetch(layer)))
+
+    factors = (
+        pltpu.make_async_copy(a_in, a_all, factor_sem.at[0]),
+        pltpu.make_async_copy(b_in, b_all, factor_sem.at[1]),
+    )
+    for copy in factors:
+        copy.start()
     load(0).start()
-
-    def fetch(i, at):
-        for j in range(col_blocks):
-            at = fetch_target(
-                i * col_blocks + j, at, total, counts, order, base, got, buffer, sem.at[i]
-            )
-        pl.when(i + 1 < row_blocks)(lambda: load(i + 1).start())
-        return at
-
-    lax.fori_loop(0, row_blocks, fetch, 0)
+    fetch_all(lambda copy: copy.start())
+    for i in range(1, row_blocks):
+        load(i).start()
     buffer[buffer.shape[0] - 1] = jnp.zeros(buffer.shape[1:], buffer.dtype)
 
     @pl.when(is_left)
@@ -957,6 +1001,8 @@
         inverse_parts[size : 2 * size] = low
         inverse_parts[2 * size :] = high
 
+    for copy in factors:
+        copy.wait()
     for k in range(b_all.shape[0]):
         cols = slice(k * lanes, (k + 1) * lanes)
         high, low = b_all[k, 0:rank, :], b_all[k, rank:, :]
@@ -967,20 +1013,38 @@
             b_cat[h * rank : (h + 1) * rank, cols] = high
             b_cat[(2 + h) * rank : (3 + h) * rank, cols] = low
 
+    def chunk(t, e):
+        picked = []
+        for k in range(STACK):
+            at = e * STACK + k
+            s = order[t * total + jnp.minimum(at, total - 1)]
+            picked.append(jnp.where(at < counts[t], s, buffer.shape[0] - 1))
+        lefts = jnp.concatenate([buffer[s, 0:rank, :] for s in picked], axis=0)
+        rights = jnp.concatenate([buffer[s, rank:, :] for s in picked], axis=0)
+        return dot(lefts, rights, ((0,), (0,)))
+
+    fetch_all(lambda copy: copy.wait())
+
     def step(i, c):
         load(i).wait()
-        for j in range(col_blocks):
-            await_target(i * col_blocks + j, counts, got, buffer, sem.at[i])
         a = jnp.concatenate([a_all[i * pieces + k] for k in range(pieces)], axis=0)
         a = jnp.concatenate([a, a], axis=1)
         a = jnp.where(jnp.logical_and(is_top, i == 0), jnp.zeros_like(a), a)
         for j in range(col_blocks):
             cols = slice(j * size, (j + 1) * size)
-            added = product(i * col_blocks + j, 0, counts, base, buffer)
+            added = chunk(i * col_blocks + j, 0)
             extended[rows(i), cols] += added - dot(a, b_cat[:, cols])
-        for j in range(col_blocks):
-            cols = slice(j * size, (j + 1) * size)
-            add_rest(i * col_blocks + j, counts, base, buffer, extended, rows(i), cols)
+
+        def more(e, c):
+            for j in range(col_blocks):
+                cols = slice(j * size, (j + 1) * size)
+                extended[rows(i), cols] += chunk(i * col_blocks + j, e)
+            return c
+
+        longest = counts[i * col_blocks]
+        for j in range(1, col_blocks):
+            longest = jnp.maximum(longest, counts[i * col_blocks + j])
+        lax.fori_loop(1, (longest + STACK - 1) // STACK, more, 0)
 
         @pl.when(jnp.logical_and(is_left, jnp.logical_not(jnp.logical_and(is_top, i == 0))))
         def _():
@@ -1009,28 +1073,28 @@
         store(i).wait()
 
 
-def finish(counts, order, got, front, a_all, b_all, pivots, upper_inverse, lower_inverse, total):
+def finish(counts, order, most, got, front, a_all, b_all, pivots, upper_inverse, lower_inverse, total):
     depth, size = got.shape[1:]
     rows, cols = front.shape
     row_blocks = rows // size
-    targets = row_blocks * (cols // size)
     return pl.pallas_call(
         functools.partial(finish_kernel, total),
         out_shape=jax.ShapeDtypeStruct(front.shape, jnp.float32),
-        in_specs=[SMEM, SMEM, HBM, HBM, VMEM, VMEM, VMEM, VMEM, VMEM],
+        in_specs=[SMEM, SMEM, SMEM, HBM, HBM, HBM, HBM, VMEM, VMEM, VMEM],
         out_specs=HBM,
         scratch_shapes=[
             pltpu.VMEM(front.shape, jnp.float32),
-            pltpu.VMEM((total + 1, depth, size), jnp.bfloat16),
+            pltpu.VMEM((got.shape[0] + 1, depth, size), jnp.bfloat16),
+            pltpu.VMEM(a_all.shape, jnp.bfloat16),
+            pltpu.VMEM(b_all.shape, jnp.bfloat16),
             pltpu.VMEM((2 * depth, cols), jnp.bfloat16),
             pltpu.VMEM((3 * size, size), jnp.bfloat16),
             pltpu.VMEM((size, size), jnp.float32),
-            pltpu.SMEM((targets,), jnp.int32),
-            DMA((row_blocks,)), DMA((row_blocks,)), DMA((row_blocks,)),
+            DMA((3,)), DMA((2,)), DMA((row_blocks,)), DMA((row_blocks,)),
         ],
         compiler_params=pltpu.CompilerParams(vmem_limit_bytes=LIMIT),
         name="finish",
-    )(counts, order, got, front, a_all, b_all, pivots, upper_inverse, lower_inverse)
+    )(counts, order, most, got, front, a_all, b_all, pivots, upper_inverse, lower_inverse)
 
 
 def shards(
@@ -1043,17 +1107,20 @@
         child_owner[:, 0], child_slot, jnp.swapaxes(child_left, 1, 2), child_right, devices
     )
     packed = packed.reshape((4, RING, RING, RING) + packed.shape[1:])
-    got, got_table = exchange(packed, table, n_row, n_col)
-    rounds = (jnp.max(got_table[:, 0, 3]) >= 0).astype(jnp.int32)
+    table = table.reshape((2, RING, RING, RING) + table.shape[1:])
+    got, got_table = exchange(packed, table, n_col)
+    got_table = got_table.reshape((devices,) + got_table.shape[3:])
+    most = jnp.max(got_table[:, 0, 0:4], axis=0)
+    rounds = (most[3] >= 0).astype(jnp.int32)
     got = lax.fori_loop(0, rounds, lambda i, g: exchange_last(packed, g, n_row, n_col), got)
     got = got.reshape((3 * devices,) + got.shape[3:])
     a_src, b_src, counts, order = panel(
-        got_table, got, front, pivots[None, :], upper_inverse, lower_inverse, column_basis.T,
+        got_table, most, got, front, pivots[None, :], upper_inverse, lower_inverse, column_basis.T,
         row_basis.T, column_ranks, row_ranks,
     )
     a_all, b_all = spread(a_src, b_src, n_row, n_col)
     return finish(
-        counts, order, got, front, a_all, b_all, pivots[None, :], upper_inverse, lower_inverse,
+        counts, order, most, got, front, a_all, b_all, pivots[None, :], upper_inverse, lower_inverse,
         devices * CAP,
     )
 

time: 227 us -> 290 us (1.28)
  the two profiles are of different devices: /device:TPU:8 before, /device:TPU:32 now
where the time goes in v3:
time: 290 us; the launch traced here: 287 us
  Pallas kernels  285 us (98%)
    pallas_call x1, Pallas kernels, exchange(): pl.pallas_call(functools.partial(exchange_kernel, n_col), out_shape=out_s...  155 us
    pallas_call x1, Pallas kernels, exchange_last(): pl.pallas_call(functools.partial(last_kernel, n_row, n_col), out_shape=(j...  59.8 us
    pallas_call x1, Pallas kernels, finish(): pl.pallas_call(functools.partial(finish_kernel, total), out_shape=jax.Sha...  23.4 us
    pallas_call x1, Pallas kernels, spread(): pl.pallas_call(functools.partial(spread_kernel, n_row, n_col), out_shape=...  21.8 us
    pallas_call x1, Pallas kernels, panel(): pl.pallas_call(functools.partial(panel_kernel, total), out_shape=(jax.Sha...  17.3 us
    pallas_call x1, Pallas kernels, pack(): pl.pallas_call(functools.partial(pack_kernel, devices), out_shape=(jax.Sh...  7.53 us

profile of v3, /device:TPU:32, one launch (start us, length us, event | category | flops | bytes accessed | tf_op | source)
XLA Modules:
  0.0 287.4 jit_solution(8129278904444483003)
XLA Ops:
  0.0 7.5 %pack.1 = (bf16[256,128,256]{2,1,0:T(8,128)(2,1)}, s32[128,1,128]{2,1,0:T(1,128)}) custom-call(s32[112]{0:T(128)} %bitcast.24, s32[1,112]{1,0:T(1,128)} %bitcast.25, s32[1,112]{1,0:T(1,128)} %bitcast.26, bf16[112,64,256]{2,1,0:T(8,128)(2,1)} %bitcast.16, bf16[112,64,256]{2,1,0:T(8,128)(2,1)} %right.1), custom_call_target="tpu_custom_call" | custom-call | tf_op jit(solution)/shard_map/pack/pallas_call | solution.py:115
  7.5 155.2 %exchange.1 = (bf16[12,4,8,128,256]{4,3,2,1,0:T(8,128)(2,1)}, s32[4,4,8,1,128]{4,3,2,1,0:T(1,128)}, bf16[8,4,4,128,256]{4,3,2,1,0:T(8,128)(2,1)}, bf16[4,8,4,128...) custom-call(bf16[4,4,4,4,128,256]{5,4,3,2,1,0:T(8,128)(2,1)} %bitcas, ...), custom_call_target="tpu_custom_call" | custom-call | tf_op jit(solution)/shard_map/exchange/pallas_call | solution.py:473
  162.7 1.0 slice_reduce_fusion.most
  163.7 0.0 copy-start
  163.7 0.6 slice.7
  164.9 0.0 copy-done
  165.0 59.9 %while.10 = (s32[]{:T(128)}, bf16[12,4,8,128,256]{4,3,2,1,0:T(8,128)(2,1)}, s32[]{:T(128)}, bf16[4,4,4,4,128,256]{5,4,3,2,1,0:T(8,128)(2,1)}, s32[]{:T(128)}) while((s32[]{:T(128)}, bf16[12,4,8,128,256]{4,3,2,1,0:T(8,128)(2,1)}, s32[]{:T(128)}, bf16[4,4,4,4,128,256]{5,4,3,2,1,0:T(8,128)(2,1)}, s32[]{:T(128)}) %tuple.21), condition=%wide.region_2.0_spmd, body=%wide.region_1.0_spmd.sunk | while | flops 2 | bytes 61 | solution.py:1115
  165.0 59.8 %exchange_last.1 = (bf16[12,4,8,128,256]{4,3,2,1,0:T(8,128)(2,1)}, bf16[128,128,256]{2,1,0:T(8,128)(2,1)}) custom-call(bf16[4,4,4,4,128,256]{5,4,3,2,1,0:T(8,128)(2,1)} %get-tuple-element.99.packed, bf16[12,4,8,128,256]{4,3,2,1,0:T(8,128)(2,1)} %get-tuple-element.92.got_in), custom_call_target="tpu_custom_call", output_to_operand_aliasing={{0}: (1, {})} | custom-call | tf_op jit(solution)/shard_map/while/body/exchange_last/pallas_call | solution.py:607
  224.8 17.3 %panel.1 = (bf16[16,128,128]{2,1,0:T(8,128)(2,1)}, bf16[8,128,128]{2,1,0:T(8,128)(2,1)}, s32[33]{0:T(128)}, s32[8704]{0:T(1024)}) custom-call(s32[128,1,128]{2,1,0:T(1,128)} %bitcast.18, s32[4]{0:T(128)} %copy-done, bf16[384,128,256]{2,1,0:T(8,128)(2,1)} %bitcast.12, f32[2048,1024]{1,0:T(8,128)} %front.3, s32[1,256]{1,0:T(1,128)} %bitcast.22, ...), custom_call_target="tpu_custom_call" | custom-call | tf_op jit(solution)/shard_map/panel/pallas_call | solution.py:823
  242.2 21.8 %spread.1 = (bf16[16,128,128]{2,1,0:T(8,128)(2,1)}, bf16[8,128,128]{2,1,0:T(8,128)(2,1)}) custom-call(bf16[16,128,128]{2,1,0:T(8,128)(2,1)} %get-tuple-element.46.a_src, bf16[8,128,128]{2,1,0:T(8,128)(2,1)} %get-tuple-element.47.b_src), custom_call_target="tpu_custom_call" | custom-call | tf_op jit(solution)/shard_map/spread/pallas_call | solution.py:937
  264.0 23.4 %finish.1 = f32[2048,1024]{1,0:T(8,128)} custom-call(s32[33]{0:T(128)} %get-tuple-element.44.counts, s32[8704]{0:T(1024)} %get-tuple-element.45.order, s32[4]{0:T(128)} %copy-done, bf16[384,128,256]{2,1,0:T(8,128)(2,1)} %bitcast.13, f32[2048,1024]{1,0:T(8,128)} %front.3, bf16[16,128,128]{2,1,0:T(8,128)(2,1)} %get-tuple-element.48.a_in, ...), custom_call_target="tpu_custom_call" | custom-call | tf_op jit(solution)/shard_map/finish/pallas_call | solution.py:1080
Async XLA Ops:
  163.7 1.2 copy-start

commit v4 on v3

--- a/solution.py
+++ b/solution.py
@@ -623,11 +623,11 @@
     base[t] = at
 
     def one(e, c):
-        pltpu.make_async_copy(got.at[order[t * total + e]], buffer.at[at + e], sem).start()
+        pltpu.make_async_copy(got.at[order[t, e]], buffer.at[at + e], sem).start()
         return c
 
-    lax.fori_loop(0, counts[t], one, 0)
-    return at + counts[t]
+    lax.fori_loop(0, counts[t, 0], one, 0)
+    return at + counts[t, 0]
 
 
 def await_target(t, counts, got, buffer, sem):
@@ -635,12 +635,12 @@
         pltpu.make_async_copy(got.at[0], buffer.at[0], sem).wait()
         return c
 
-    lax.fori_loop(0, counts[t], one, 0)
+    lax.fori_loop(0, counts[t, 0], one, 0)
 
 
 def product(t, e, counts, base, buffer):
     rank = buffer.shape[1] // 2
-    n, begin = counts[t], base[t]
+    n, begin = counts[t, 0], base[t]
     picked = [
         jnp.where(e * STACK + k < n, begin + e * STACK + k, buffer.shape[0] - 1) for k in range(STACK)
     ]
@@ -654,12 +654,18 @@
         sum_ref[rows, cols] += product(t, e, counts, base, buffer)
         return c
 
-    lax.fori_loop(1, (counts[t] + STACK - 1) // STACK, chunk, 0)
+    lax.fori_loop(1, (counts[t, 0] + STACK - 1) // STACK, chunk, 0)
 
 
 def split(x):
     high = x.astype(jnp.bfloat16)
     return high, (x - high.astype(jnp.float32)).astype(jnp.bfloat16)
+
+
+def dot3(a, b):
+    a_high, a_low = split(a)
+    b_high, b_low = split(b)
+    return dot(a_high, b_high) + (dot(a_high, b_low) + dot(a_low, b_high))
 
 
 def permutation(pivots):
@@ -669,54 +675,53 @@
 
 
 def panel_kernel(
-    total, table, most, got, front, pivots, upper_inverse, lower_inverse, column_basis, row_basis,
+    total, table, got, front, pivots, upper_inverse, lower_inverse, column_basis, row_basis,
     column_ranks, row_ranks, a_out, b_out, counts, order, left_sum, top_sum, buffer, top_weights,
-    left_weights, coupling, base, sem, front_sem,
+    left_weights, coupling, order_rows, count_rows, base, sem, front_sem, sort_sem,
 ):
     size, rank = upper_inverse.shape[0], column_basis.shape[0]
     row_blocks, col_blocks = front.shape[0] // size, front.shape[1] // size
     targets = row_blocks * col_blocks
-    devices = table.shape[0]
+    devices = total // CAP
     is_top, is_left = lax.axis_index("row") == 0, lax.axis_index("col") == 0
     load_left = pltpu.make_async_copy(front.at[:, pl.ds(0, size)], left_sum, front_sem.at[0])
     load_top = pltpu.make_async_copy(front.at[pl.ds(0, size)], top_sum, front_sem.at[1])
     pl.when(is_left)(load_left.start)
     pl.when(is_top)(load_top.start)
 
-    for t in range(targets + 1):
-        counts[t] = 0
-
-    def note(s, p, at):
-        t = table[s, 0, p]
-        t = jnp.where(t < 0, targets, t)
-        n = counts[t]
-        order[t * total + n] = at
-        counts[t] = n + 1
-
     core = lax.rem(lax.axis_index("col"), 2)
-    w_high, w_middle, w_low = 1 + core * 3, 16 - core * 15, 4 + core * 12
-
-    def digits(k):
-        return k // 32, lax.rem(k // 8, 4), lax.rem(k // 2, 4), lax.rem(k, 2)
-
-    def tally(k, c):
-        note(k, 0, k)
-        return c
-
-    def tally_shared(k, c):
-        high, middle, low, side = digits(k)
-        note(k, 1, devices + side * CHIPS + high * w_high + middle * w_middle + low * w_low)
-        return c
-
-    def tally_last(k, c):
-        high, middle, low, side = digits(k)
-        x, y, z = (jnp.where(core == 0, a, b) for a, b in ((low, high), (middle, low), (high, middle)))
-        note(k, 2, 2 * devices + x * 32 + lax.rem(z, 2) * 16 + y * 4 + (z // 2) * 2 + side)
-        return c
-
-    lax.fori_loop(0, devices, tally, 0, unroll=8)
-    lax.fori_loop(0, jnp.where(most[1] >= 0, devices, 0), tally_shared, 0)
-    lax.fori_loop(0, jnp.where(most[2] >= 0, devices, 0), tally_last, 0)
+    k = lax.broadcasted_iota(jnp.int32, (1, devices), 1)
+    high, middle, low, side = k >> 5, (k >> 3) & 3, (k >> 1) & 3, k & 1
+    x, y, z = (jnp.where(core == 0, a, b) for a, b in ((low, high), (middle, low), (high, middle)))
+    shared = devices + side * CHIPS + y * 16 + x * 4 + z
+    last = 2 * devices + x * 32 + (z & 1) * 16 + y * 4 + (z & 2) + side
+    block = jnp.concatenate([k, shared, last], axis=1)
+    target = jnp.concatenate([table[p : p + 1, :] for p in range(3)], axis=1)
+    entries = block.shape[1]
+    member = lax.broadcasted_iota(jnp.int32, (targets, entries), 0) == target
+    member_one = member.astype(jnp.float32)
+    before = (
+        lax.broadcasted_iota(jnp.int32, (entries, entries), 0)
+        < lax.broadcasted_iota(jnp.int32, (entries, entries), 1)
+    ).astype(jnp.bfloat16)
+    earlier = dot(member_one.astype(jnp.bfloat16), before)
+    rank_of = jnp.sum(jnp.where(member, earlier, 0.0), axis=0, keepdims=True)
+    chosen = lax.broadcasted_iota(jnp.int32, (total, entries), 0) == rank_of.astype(jnp.int32)
+    upper_part = jnp.where(member, (block >> 7).astype(jnp.float32), 0.0).astype(jnp.bfloat16)
+    lower_part = jnp.where(member, (block & 127).astype(jnp.float32), 0.0).astype(jnp.bfloat16)
+    chosen = chosen.astype(jnp.float32).astype(jnp.bfloat16)
+    listed = dot(upper_part, chosen, ((1,), (1,))) * 128.0 + dot(lower_part, chosen, ((1,), (1,)))
+    order_rows[...] = listed.astype(jnp.int32)
+    tally = jnp.sum(member_one, axis=1, keepdims=True).astype(jnp.int32)
+    count_rows[...] = jnp.broadcast_to(tally, count_rows.shape)
+    copies = (
+        pltpu.make_async_copy(order_rows, order, sort_sem.at[0]),
+        pltpu.make_async_copy(count_rows, counts, sort_sem.at[1]),
+    )
+    for copy in copies:
+        copy.start()
+    for copy in copies:
+        copy.wait()
 
     @pl.when(jnp.logical_or(is_top, is_left))
     def _():
@@ -773,7 +778,7 @@
             add_rest(j, counts, base, buffer, top_sum, slice(0, size), slice(j * size, (j + 1) * size))
         for j in range(col_blocks):
             cols = slice(j * size, (j + 1) * size)
-            factor = dot(top_weights[...], top_sum[:, cols], precision=HIGHEST)
+            factor = dot3(top_weights[...], top_sum[:, cols])
             factor = jnp.where(lax.rem(row, rank) < row_ranks[j], factor, 0.0)
             high, low = split(factor)
             value = jnp.where(row < rank, high.astype(jnp.float32), low.astype(jnp.float32))
@@ -801,9 +806,9 @@
 
         def block(i, c):
             rows = pl.ds(pl.multiple_of(i * size, size), size)
-            factor = dot(left_sum[rows, :], left_weights[...], precision=HIGHEST)
+            factor = dot3(left_sum[rows, :], left_weights[...])
             factor = jnp.where(lane[:, 0:rank] < column_ranks[i], factor, 0.0)
-            high, low = split(dot(factor, coupling[...], precision=HIGHEST))
+            high, low = split(dot3(factor, coupling[...]))
             value = jnp.where(lane < rank, high.astype(jnp.float32), low.astype(jnp.float32))
             for h in range(size // 128):
                 a_out[i * (size // 128) + h] = value[h * 128 : (h + 1) * 128].astype(jnp.bfloat16)
@@ -813,11 +818,11 @@
 
 
 def panel(
-    table, most, got, front, pivots, upper_inverse, lower_inverse, column_basis, row_basis, column_ranks,
+    table, got, front, pivots, upper_inverse, lower_inverse, column_basis, row_basis, column_ranks,
     row_ranks,
 ):
     depth, size = got.shape[1:]
-    total = table.shape[0] * CAP
+    total = table.shape[1] * CAP
     rows, cols = front.shape
     targets = (rows // size) * (cols // size)
     return pl.pallas_call(
@@ -825,10 +830,10 @@
         out_shape=(
             jax.ShapeDtypeStruct((rows // 128, 128, 128), jnp.bfloat16),
             jax.ShapeDtypeStruct((cols // 128, 128, 128), jnp.bfloat16),
-            jax.ShapeDtypeStruct((targets + 1,), jnp.int32),
-            jax.ShapeDtypeStruct(((targets + 2) * total,), jnp.int32),
+            jax.ShapeDtypeStruct((targets, 128), jnp.int32),
+            jax.ShapeDtypeStruct((targets, total), jnp.int32),
         ),
-        in_specs=[SMEM, SMEM, HBM, HBM, VMEM, VMEM, VMEM, VMEM, VMEM, SMEM, SMEM],
+        in_specs=[VMEM, HBM, HBM, VMEM, VMEM, VMEM, VMEM, VMEM, SMEM, SMEM],
         out_specs=(VMEM, VMEM, SMEM, SMEM),
         scratch_shapes=[
             pltpu.VMEM((rows, size), jnp.float32),
@@ -837,14 +842,17 @@
             pltpu.VMEM((depth, size), jnp.float32),
             pltpu.VMEM((size, depth // 2), jnp.float32),
             pltpu.VMEM((depth // 2, depth), jnp.float32),
+            pltpu.VMEM((targets, total), jnp.int32),
+            pltpu.VMEM((targets, 128), jnp.int32),
             pltpu.SMEM((targets,), jnp.int32),
             DMA,
+            DMA((2,)),
             DMA((2,)),
         ],
         compiler_params=pltpu.CompilerParams(vmem_limit_bytes=LIMIT),
         name="panel",
     )(
-        table, most, got, front, pivots, upper_inverse, lower_inverse, column_basis, row_basis,
+        table, got, front, pivots, upper_inverse, lower_inverse, column_basis, row_basis,
         column_ranks, row_ranks,
     )
 
@@ -940,8 +948,8 @@
             jax.ShapeDtypeStruct(a_src.shape, a_src.dtype),
             jax.ShapeDtypeStruct(b_src.shape, b_src.dtype),
         ),
-        in_specs=[HBM, HBM],
-        out_specs=(HBM, HBM),
+        in_specs=[VMEM, VMEM],
+        out_specs=(VMEM, VMEM),
         scratch_shapes=[
             DMA((n_col,)), DMA, DMA((n_row,)), DMA,
             DMA((n_col // 2,)), DMA((n_col // 2,)), DMA((n_row,)), DMA((n_row,)), DMA((2,)), DMA((2,)),
@@ -988,10 +996,9 @@
     )
     for copy in factors:
         copy.start()
-    load(0).start()
+    for i in range(row_blocks):
+        load(i).start()
     fetch_all(lambda copy: copy.start())
-    for i in range(1, row_blocks):
-        load(i).start()
     buffer[buffer.shape[0] - 1] = jnp.zeros(buffer.shape[1:], buffer.dtype)
 
     @pl.when(is_left)
@@ -1017,34 +1024,36 @@
         picked = []
         for k in range(STACK):
             at = e * STACK + k
-            s = order[t * total + jnp.minimum(at, total - 1)]
-            picked.append(jnp.where(at < counts[t], s, buffer.shape[0] - 1))
+            s = order[t, jnp.minimum(at, total - 1)]
+            picked.append(jnp.where(at < counts[t, 0], s, buffer.shape[0] - 1))
         lefts = jnp.concatenate([buffer[s, 0:rank, :] for s in picked], axis=0)
         rights = jnp.concatenate([buffer[s, rank:, :] for s in picked], axis=0)
         return dot(lefts, rights, ((0,), (0,)))
 
-    fetch_all(lambda copy: copy.wait())
-
-    def step(i, c):
+    def update(i, c):
         load(i).wait()
         a = jnp.concatenate([a_all[i * pieces + k] for k in range(pieces)], axis=0)
         a = jnp.concatenate([a, a], axis=1)
         a = jnp.where(jnp.logical_and(is_top, i == 0), jnp.zeros_like(a), a)
         for j in range(col_blocks):
             cols = slice(j * size, (j + 1) * size)
-            added = chunk(i * col_blocks + j, 0)
-            extended[rows(i), cols] += added - dot(a, b_cat[:, cols])
-
+            extended[rows(i), cols] -= dot(a, b_cat[:, cols])
+        return c
+
+    lax.fori_loop(0, row_blocks, update, 0)
+    fetch_all(lambda copy: copy.wait())
+
+    def step(i, c):
         def more(e, c):
             for j in range(col_blocks):
                 cols = slice(j * size, (j + 1) * size)
                 extended[rows(i), cols] += chunk(i * col_blocks + j, e)
             return c
 
-        longest = counts[i * col_blocks]
+        longest = counts[i * col_blocks, 0]
         for j in range(1, col_blocks):
-            longest = jnp.maximum(longest, counts[i * col_blocks + j])
-        lax.fori_loop(1, (longest + STACK - 1) // STACK, more, 0)
+            longest = jnp.maximum(longest, counts[i * col_blocks + j, 0])
+        lax.fori_loop(0, (longest + STACK - 1) // STACK, more, 0)
 
         @pl.when(jnp.logical_and(is_left, jnp.logical_not(jnp.logical_and(is_top, i == 0))))
         def _():
@@ -1110,12 +1119,13 @@
     table = table.reshape((2, RING, RING, RING) + table.shape[1:])
     got, got_table = exchange(packed, table, n_col)
     got_table = got_table.reshape((devices,) + got_table.shape[3:])
-    most = jnp.max(got_table[:, 0, 0:4], axis=0)
+    lines = got_table[:, 0, 0:8].T
+    most = jnp.max(lines, axis=1)
     rounds = (most[3] >= 0).astype(jnp.int32)
     got = lax.fori_loop(0, rounds, lambda i, g: exchange_last(packed, g, n_row, n_col), got)
     got = got.reshape((3 * devices,) + got.shape[3:])
     a_src, b_src, counts, order = panel(
-        got_table, most, got, front, pivots[None, :], upper_inverse, lower_inverse, column_basis.T,
+        lines, got, front, pivots[None, :], upper_inverse, lower_inverse, column_basis.T,
         row_basis.T, column_ranks, row_ranks,
     )
     a_all, b_all = spread(a_src, b_src, n_row, n_col)

time: 290 us -> 224 us (0.77)
  Pallas kernels: 285 us -> 220 us
    pallas_call x1 -> x0, Pallas kernels: 59.8 us -> none  [exchange_last(): pl.pallas_call(functools.partial(last_kernel, n_row, n_col), out_shape=(j...]
    pallas_call x1, Pallas kernels: 17.3 us -> 12.3 us  [panel(): pl.pallas_call(functools.partial(panel_kernel, total), out_shape=(jax.Sha...]
where the time goes in v4:
time: 224 us; the launch traced here: 223 us
  Pallas kernels  220 us (98%)
    pallas_call x1, Pallas kernels, exchange(): pl.pallas_call(functools.partial(exchange_kernel, n_col), out_shape=out_s...  155 us
    pallas_call x1, Pallas kernels, finish(): pl.pallas_call(functools.partial(finish_kernel, total), out_shape=jax.Sha...  24.9 us
    pallas_call x1, Pallas kernels, spread(): pl.pallas_call(functools.partial(spread_kernel, n_row, n_col), out_shape=...  20.2 us
    pallas_call x1, Pallas kernels, panel(): pl.pallas_call(functools.partial(panel_kernel, total), out_shape=(jax.Sha...  12.3 us
    pallas_call x1, Pallas kernels, pack(): pl.pallas_call(functools.partial(pack_kernel, devices), out_shape=(jax.Sh...  7.47 us

profile of v4, /device:TPU:32, one launch (start us, length us, event | category | flops | bytes accessed | tf_op | source)
XLA Modules:
  0.0 223.0 jit_solution(3543092551532949433)
XLA Ops:
  0.0 7.5 %pack.1 = (bf16[256,128,256]{2,1,0:T(8,128)(2,1)}, s32[128,1,128]{2,1,0:T(1,128)}) custom-call(s32[112]{0:T(128)} %bitcast.27, s32[1,112]{1,0:T(1,128)} %bitcast.28, s32[1,112]{1,0:T(1,128)} %bitcast.29, bf16[112,64,256]{2,1,0:T(8,128)(2,1)} %bitcast.19, bf16[112,64,256]{2,1,0:T(8,128)(2,1)} %right.1), custom_call_target="tpu_custom_call" | custom-call | tf_op jit(solution)/shard_map/pack/pallas_call | solution.py:115
  7.5 155.2 %exchange.1 = (bf16[12,4,8,128,256]{4,3,2,1,0:T(8,128)(2,1)}, s32[4,4,8,1,128]{4,3,2,1,0:T(1,128)}, bf16[8,4,4,128,256]{4,3,2,1,0:T(8,128)(2,1)}, bf16[4,8,4,128...) custom-call(bf16[4,4,4,4,128,256]{5,4,3,2,1,0:T(8,128)(2,1)} %bitcas, ...), custom_call_target="tpu_custom_call" | custom-call | tf_op jit(solution)/shard_map/exchange/pallas_call | solution.py:473
  162.7 0.9 slice_reduce_fusion
  163.6 0.0 copy-start
  163.6 0.6 slice.7
  164.8 0.0 copy-done
  164.8 0.7 copy.16
  165.5 12.3 %panel.1 = (bf16[16,128,128]{2,1,0:T(8,128)(2,1)}, bf16[8,128,128]{2,1,0:T(8,128)(2,1)}, s32[32,128]{1,0:T(8,128)}, s32[32,256]{1,0:T(8,128)}) custom-call(s32[8,128]{1,0:T(8,128)} %bitcast.24, bf16[384,128,256]{2,1,0:T(8,128)(2,1)} %bitcast.15, f32[2048,1024]{1,0:T(8,128)} %front.3, s32[1,256]{1,0:T(1,128)} %bitcast.25, f32[256,256]{1,0:T(8,128)} %upper_inverse.3, ...), custom_call_target="tpu_custom_call" | custom-call | tf_op jit(solution)/shard_map/panel/pallas_call | solution.py:828
  177.8 20.2 %spread.1 = (bf16[16,128,128]{2,1,0:T(8,128)(2,1)}, bf16[8,128,128]{2,1,0:T(8,128)(2,1)}) custom-call(bf16[16,128,128]{2,1,0:T(8,128)(2,1)} %get-tuple-element.46.a_src, bf16[8,128,128]{2,1,0:T(8,128)(2,1)} %get-tuple-element.47.b_src), custom_call_target="tpu_custom_call" | custom-call | tf_op jit(solution)/shard_map/spread/pallas_call | solution.py:945
  198.0 24.9 %finish.1 = f32[2048,1024]{1,0:T(8,128)} custom-call(s32[32,128]{1,0:T(8,128)} %get-tuple-element.44.counts, s32[32,256]{1,0:T(8,128)} %get-tuple-element.45.order, s32[8]{0:T(128)} %copy-done, bf16[384,128,256]{2,1,0:T(8,128)(2,1)} %bitcast.16, f32[2048,1024]{1,0:T(8,128)} %front.3, bf16[16,128,128]{2,1,0:T(8,128)(2,1)} %get-tuple-element.48.a_in, ...), custom_call_target="tpu_custom_call" | custom-call | tf_op jit(solution)/shard_map/finish/pallas_call | solution.py:1089
  (1 shorter events, 0.0 us)
Async XLA Ops:
  163.6 1.2 copy-start
